TPU v7x, 512 devices: a whole 4x8x8 slice. The times are simulated.
512 devices in a mesh: seq: 64 (over x, z, core), tp: 8 (over y).
Axes of the slice: x: 4, y: 8, z: 8, core: 2. Of those that a mesh axis runs over, the one named last changes fastest.
Arguments:
- tokens: bfloat16 [16384, 4096], P('seq', 'tp'), may hold values from -6 to 6
- in_weight: bfloat16 [3, 4096, 2048], P(None, 'seq', 'tp'), may hold values from -0.09375 to 0.09375
- short_taps: float32 [3, 3, 2048], P(None, None, 'tp'), may hold values from -3.5 to 3.5
- long_filter: float32 [16384, 2048], P('seq', 'tp'), may hold values from -1.3 to 1.3
- skip: float32 [2048], P('tp'), may hold values from -4 to 4
- out_weight: bfloat16 [2048, 4096], P('tp'), may hold values from -0.125 to 0.125
Outputs:
- layer_out: bfloat16 [16384, 4096], P('seq', 'tp')
All inputs are finite; a program needn't handle non-finite values.
Results may differ from a plain program's by a relative error of at most 0.0049.
Values may be sent and summed in bfloat16 or wider, within the bound.
No kernel may reach another device: no remote copies, remote signals or barrier semaphores. Data moves between devices by JAX's collectives and lax.ppermute only.
A program may use at most 64 MiB of HBM per device.

v0:
```python
import functools
import math

import jax
import jax.numpy as jnp
import ml_dtypes
import numpy as np
from jax import lax
from jax.experimental import pallas as pl
from jax.experimental.pallas import tpu as pltpu
from jax.sharding import PartitionSpec as P

SIDE = 128
BF = jnp.bfloat16


def split_table(table):
    high = table.astype(np.float32).astype(ml_dtypes.bfloat16)
    low = (table - high.astype(np.float64)).astype(np.float32).astype(ml_dtypes.bfloat16)
    return np.stack([high, low])


@functools.cache
def tables():
    length = 2 * SIDE * SIDE
    ids = np.arange(SIDE)
    first = 2 * math.pi * np.outer(ids + 0.5, ids) / (2 * SIDE)
    turn = 2 * math.pi * np.outer(ids + 0.5, ids) / length
    second = 2 * math.pi * (np.outer(ids, ids) % SIDE) / SIDE
    columns = np.concatenate([np.cos(first), -np.sin(first)], axis=0)
    cos_two, sin_two = np.cos(second), np.sin(second)
    forward = np.block([[cos_two, -sin_two], [sin_two, cos_two]])
    backward = np.block([[cos_two, sin_two], [-sin_two, cos_two]])
    twist = np.stack([np.cos(turn), np.sin(turn)]).astype(np.float32)
    return (
        split_table(columns),
        split_table(columns.T * (2.0 / length)),
        split_table(forward),
        split_table(backward),
        twist,
    )


def halves(value):
    high = value.astype(BF)
    return high, (value - high.astype(jnp.float32)).astype(BF)


def mm(left, right):
    return jnp.dot(left, right, preferred_element_type=jnp.float32)


def table_times(table, value):
    high, low = halves(value)
    return mm(table[0], high) + (mm(table[1], high) + mm(table[0], low))


def times_table(value, table):
    high, low = halves(value)
    return mm(high, table[0]) + (mm(high, table[1]) + mm(low, table[0]))


def spectrum(block, columns, forward, cosine, sine):
    first = table_times(columns, block)
    real, imag = first[:SIDE], first[SIDE:]
    turned = jnp.concatenate([real * cosine + imag * sine, imag * cosine - real * sine], axis=1)
    return times_table(turned, forward)


def filter_kernel(filter_ref, columns_ref, forward_ref, twist_ref, out_ref):
    columns = (columns_ref[0], columns_ref[1])
    forward = (forward_ref[0], forward_ref[1])
    for channel in range(filter_ref.shape[0]):
        out_ref[channel] = spectrum(
            filter_ref[channel], columns, forward, twist_ref[0], twist_ref[1]
        )


def conv_kernel(source_ref, spec_ref, columns_ref, rows_ref, forward_ref, backward_ref, twist_ref, out_ref):
    columns = (columns_ref[0], columns_ref[1])
    rows = (rows_ref[0], rows_ref[1])
    forward = (forward_ref[0], forward_ref[1])
    backward = (backward_ref[0], backward_ref[1])
    cosine, sine = twist_ref[0], twist_ref[1]
    for channel in range(source_ref.shape[0]):
        signal = spectrum(
            source_ref[channel].astype(jnp.float32), columns, forward, cosine, sine
        )
        sig_real, sig_imag = signal[:, :SIDE], signal[:, SIDE:]
        taps = spec_ref[channel]
        tap_real, tap_imag = taps[:, :SIDE], taps[:, SIDE:]
        product = jnp.concatenate(
            [sig_real * tap_real - sig_imag * tap_imag, sig_real * tap_imag + sig_imag * tap_real],
            axis=1,
        )
        back = times_table(product, backward)
        real, imag = back[:, :SIDE], back[:, SIDE:]
        turned = jnp.concatenate([real * cosine - imag * sine, imag * cosine + real * sine], axis=0)
        out_ref[channel] = table_times(rows, turned).astype(out_ref.dtype)


def filter_spectrum(blocks):
    columns, _, forward, _, twist = (jnp.asarray(table) for table in tables())
    count = blocks.shape[0]
    return pl.pallas_call(
        filter_kernel,
        out_shape=jax.ShapeDtypeStruct((count, SIDE, 2 * SIDE), jnp.float32),
        compiler_params=pltpu.CompilerParams(vmem_limit_bytes=16 * 2**20),
    )(blocks, columns, forward, twist)


def long_convolution(blocks, spec):
    columns, rows, forward, backward, twist = (jnp.asarray(table) for table in tables())
    return pl.pallas_call(
        conv_kernel,
        out_shape=jax.ShapeDtypeStruct(blocks.shape, BF),
        compiler_params=pltpu.CompilerParams(vmem_limit_bytes=16 * 2**20),
    )(blocks, spec, columns, rows, forward, backward, twist)


def body(groups, tokens, in_weight, short_taps, long_filter, skip, out_weight):
    x_groups, z_groups, core_groups, chip_groups = groups
    seq_count = lax.axis_size("seq")
    tp_count = lax.axis_size("tp")
    seq_index = lax.axis_index("seq")
    core = seq_index % 2
    chips = seq_count // 2
    rows = tokens.shape[0]
    depth = in_weight.shape[1]
    half = in_weight.shape[2] // 2
    own = half // chips

    def exchange(value, axis, members):
        return lax.all_to_all(
            value, axis, split_axis=0, concat_axis=0, tiled=True, axis_index_groups=members
        )

    def swap(value):
        return lax.ppermute(value, "seq", [(i, i ^ 1) for i in range(seq_count)])

    mine = lax.all_gather(tokens, "tp", axis=1, tiled=True)
    theirs = swap(mine)

    weights = in_weight.reshape(3, depth, 2, half).transpose(2, 1, 0, 3).reshape(2, depth, 3 * half)
    weights = exchange(weights, "seq", core_groups).reshape(1, 2 * depth, 3 * half)
    for members in (z_groups, x_groups):
        count = len(members[0])
        weights = exchange(
            jnp.broadcast_to(weights, (count,) + weights.shape[1:]), "seq", members
        ).reshape(1, -1, 3 * half)
    weights = weights[0]

    filter_in = long_filter.T.reshape(2, chips, own, rows).transpose(1, 0, 2, 3)
    filter_in = exchange(filter_in.reshape(seq_count, own, rows), "seq", None)
    filter_in = filter_in.transpose(1, 0, 2).reshape(own, SIDE, SIDE)
    spec = filter_spectrum(filter_in)

    piece = out_weight.shape[0] // seq_count
    out_columns = out_weight.shape[1] // tp_count
    wanted = lax.dynamic_slice_in_dim(out_weight, seq_index * piece, piece, 0)
    wanted = exchange(wanted.reshape(piece, tp_count, out_columns).transpose(1, 0, 2), "tp", None)
    wanted = lax.all_gather(wanted, "seq", axis=0)
    wanted = wanted.transpose(1, 0, 2, 3).reshape(-1, out_columns)

    def project(value):
        return jnp.dot(value, weights, preferred_element_type=jnp.float32)

    projected_mine, projected_theirs = project(mine), project(theirs)
    is_first = core == 0
    projected = jnp.concatenate(
        [
            jnp.where(is_first, projected_mine, projected_theirs),
            jnp.where(is_first, projected_theirs, projected_mine),
        ],
        axis=0,
    )
    chip_rows = 2 * rows
    rim = short_taps.shape[0] - 1
    before = lax.ppermute(
        projected[chip_rows - rim :], "seq", [(i, i + 2) for i in range(seq_count - 2)]
    )
    extended = jnp.concatenate([before, projected], axis=0)
    taps = lax.dynamic_slice_in_dim(short_taps, core * half, half, 2).reshape(rim + 1, 1, 3 * half)
    mixed = sum(
        taps[offset] * extended[rim - offset : rim - offset + chip_rows] for offset in range(rim + 1)
    )
    mixed = mixed.T.reshape(3, half, chip_rows)
    source = mixed[1] * mixed[0]

    blocks = exchange(source.astype(BF).reshape(chips, own, chip_rows), "seq", chip_groups)
    blocks = blocks.transpose(1, 0, 2).reshape(own, SIDE, SIDE)
    result = long_convolution(blocks, spec)
    result = result.reshape(own, chips, chip_rows).transpose(1, 0, 2)
    long_conv = exchange(result, "seq", chip_groups).reshape(half, chip_rows)

    own_skip = lax.dynamic_slice_in_dim(skip, core * half, half, 0)
    gated = (mixed[2] * (long_conv.astype(jnp.float32) + own_skip[:, None] * source)).astype(BF)
    gated = exchange(gated.reshape(half, 2, rows).transpose(1, 0, 2), "seq", core_groups)
    gated = gated.reshape(1, 2 * half, rows)
    gated = exchange(jnp.broadcast_to(gated, (tp_count,) + gated.shape[1:]), "tp", None)
    gated = gated.reshape(-1, rows)
    out = lax.dot_general(
        gated, wanted, (((0,), (0,)), ((), ())), preferred_element_type=jnp.float32
    )
    return out.astype(BF)


def solution(mesh):
    width, depth = 4, 8
    place = lambda x, z, c: (x * depth + z) * 2 + c
    x_groups = [[place(x, z, c) for x in range(width)] for z in range(depth) for c in range(2)]
    z_groups = [[place(x, z, c) for z in range(depth)] for x in range(width) for c in range(2)]
    core_groups = [[place(x, z, c) for c in range(2)] for x in range(width) for z in range(depth)]
    chip_groups = [
        [place(x, z, c) for x in range(width) for z in range(depth)] for c in range(2)
    ]
    return jax.shard_map(
        functools.partial(body, (x_groups, z_groups, core_groups, chip_groups)),
        mesh=mesh,
        in_specs=(
            P("seq", "tp"),
            P(None, "seq", "tp"),
            P(None, None, "tp"),
            P("seq", "tp"),
            P("tp"),
            P("tp", None),
        ),
        out_specs=P("seq", "tp"),
        check_vma=False,
    )
```

profile of v0, /device:TPU:1, one launch (start us, length us, event | category | flops | bytes accessed | tf_op | source)
XLA Modules:
  0.0 212.6 jit_solution(10943104267170640245)
XLA Ops:
  7.4 0.7 all-gather.4.cloned.1.call-update
  8.1 0.9 reshape.73
  9.0 0.1 copy.77
  9.1 0.7 reshape.74
  9.8 10.2 %all-to-all-start = ((bf16[2,64,384]{2,1,0:T(8,128)(2,1)}), bf16[2,64,384]{2,1,0:T(8,128)(2,1)S(1)}, u32[]{:S(2)}, u32[]{:S(2)}) async-start(bf16[2,64,384]{2,1,0:T(8,128)(2,1)} %reshape.74), calls=%async_computation | async-start | bytes 196608 | tf_op jit(solution)/shard_map/all_to_all | solution.py:134
  20.1 1.1 all-to-all-done
  21.1 9.2 %all_to_all.45 = bf16[8,4,512]{2,1,0:T(4,128)(2,1)S(1)} all-to-all(bf16[8,4,512]{2,1,0:T(4,128)(2,1)S(1)} %bitcast.51), channel_id=1, replica_groups=mesh['seq'=64,'tp'=8] {'tp'}, dimensions={0} | all-to-all | bytes 65536 | tf_op jit(solution)/shard_map/all_to_all | solution.py:134
  30.4 29.0 %all_to_all.46 = bf16[8,128,384]{2,1,0:T(8,128)(2,1)S(1)} all-to-all(bf16[8,128,384]{2,1,0:T(8,128)(2,1)S(1)} %broadcast_in_dim.23), channel_id=1, replica_groups={{0,16,32,48,64,80,96,112},{8,24,40,56,72,88,104,120},{128,144,160,176,1..., dimensions={0} | all-to-all | bytes 1572864 | tf_op jit(solution)/shard_map/all_to_all | solution.py:134
  59.4 2.0 broadcast_in_dim.25
  61.4 4.8 %all-to-all-start.2 = ((bf16[4,1024,384]{2,1,0:T(8,128)(2,1)}), bf16[4,1024,384]{2,1,0:T(8,128)(2,1)}, u32[]{:S(2)}, u32[]{:S(2)}) async-start(bf16[4,1024,384]{2,1,0:T(8,128)(2,1)} %broadcast_in_dim.25), calls=%async_computation.2 | async-start | bytes 6291456 | tf_op jit(solution)/shard_map/all_to_all | solution.py:134
  66.2 5.8 %collective-permute-start = (bf16[256,4096]{1,0:T(8,128)(2,1)}, bf16[256,4096]{1,0:T(8,128)(2,1)}, u32[]{:S(2)}, u32[]{:S(2)}) collective-permute-start(bf16[256,4096]{1,0:T(8,128)(2,1)} %all-gather.4.cloned.1.call-done), channel_id=1, source_target_pairs={{0,8},{8,0},{16,24},{24,16},{32,40},{40,32},{48,56},{56,48},{64,72... | collective-permute-start | bytes 6291464 | tf_op jit(solution)/shard_map/ppermute | solution.py:139
  72.1 0.1 copy.58
  72.2 0.1 reshape.76
  72.3 0.7 copy.59
  73.0 0.6 copy.65
  73.6 26.8 %all-to-all-done.2 = bf16[4,1024,384]{2,1,0:T(8,128)(2,1)} async-done(((bf16[4,1024,384]{2,1,0:T(8,128)(2,1)}), bf16[4,1024,384]{2,1,0:T(8,128)(2,1)}, u32[]{:S(2)}, u32[]{:S(2)}) %all-to-all-start.2) | async-done | bytes 3145760 | tf_op jit(solution)/shard_map/all_to_all | solution.py:134
  100.5 9.7 %all-to-all-start.4 = ((f32[64,4,256]{2,1,0:T(4,128)}), f32[64,4,256]{2,1,0:T(4,128)S(1)}, u32[]{:S(2)}, u32[]{:S(2)}) async-start(f32[64,4,256]{2,1,0:T(4,128)} %bitcast.12), calls=%async_computation.4 | async-start | bytes 524288 | tf_op jit(solution)/shard_map/all_to_all | solution.py:134
  110.2 3.8 %fusion.7 = f32[256,384]{1,0:T(8,128)S(1)} fusion(bf16[256,4096]{1,0:T(8,128)(2,1)} %all-gather.4.cloned.1.call-done, bf16[4096,384]{1,0:T(8,128)(2,1)} %bitcast.4), kind=kOutput, calls=%fused_computation.22 | convolution fusion | flops 805306368 | bytes 5636096 | tf_op jit(solution)/shard_map/dot_general | solution.py:166
  114.1 3.8 %broadcast_select_fusion.1 = (f32[256,384]{1,0:T(8,128)S(1)}, f32[256,384]{1,0:T(8,128)S(1)}) fusion(f32[256,384]{1,0:T(8,128)S(1)} %fusion.7, pred[]{:T(512)S(6)} %eq.5, bf16[256,4096]{1,0:T(8,128)(2,1)} %collective-permute-done, bf16[4096,384]{1,0:T(8,128)(2,1)} %bitcast.4), kind=kOutput, calls=%fused_computation.13 | convolution fusion | flops 805502976 | bytes 6422529 | tf_op jit(solution)/shard_map/dot_general | solution.py:166
  117.9 3.3 %collective-permute-start.1 = (f32[2,384]{1,0:T(2,128)S(1)}, f32[2,384]{1,0:T(2,128)S(1)}, u32[]{:S(2)}, u32[]{:S(2)}) collective-permute-start(f32[2,384]{1,0:T(2,128)S(1)} %slice.42), channel_id=1, source_target_pairs={{0,16},{8,24},{16,32},{24,40},{32,48},{40,56},{48,64},{56,72},{64,... | collective-permute-start | bytes 9224 | tf_op jit(solution)/shard_map/ppermute | solution.py:179
  121.2 0.7 collective-permute-done.1
  122.0 0.2 fusion.1
  122.2 0.8 fusion.6
  123.0 0.1 copy.56
  123.2 0.7 convert_element_type.22
  123.9 11.2 %all-to-all-start.3 = ((bf16[32,4,512]{2,1,0:T(4,128)(2,1)}), bf16[32,4,512]{2,1,0:T(4,128)(2,1)}, u32[]{:S(2)}, u32[]{:S(2)}) async-start(bf16[32,4,512]{2,1,0:T(4,128)(2,1)} %convert_element_type.22), calls=%async_computation.3 | async-start | bytes 262144 | tf_op jit(solution)/shard_map/all_to_all | solution.py:134
  135.2 0.8 shard_map.109.spec_ref
  135.9 9.3 %all-to-all-done.3 = bf16[32,4,512]{2,1,0:T(4,128)(2,1)} async-done(((bf16[32,4,512]{2,1,0:T(4,128)(2,1)}), bf16[32,4,512]{2,1,0:T(4,128)(2,1)}, u32[]{:S(2)}, u32[]{:S(2)}) %all-to-all-start.3) | async-done | bytes 131104 | tf_op jit(solution)/shard_map/all_to_all | solution.py:134
  145.2 0.9 copy.57
  146.1 0.1 reshape.75.source_ref
  146.2 0.9 copy-done.4
  147.2 2.4 %shard_map.110 = bf16[4,128,128]{2,1,0:T(8,128)(2,1)S(1)} custom-call(bf16[4,128,128]{2,1,0:T(8,128)(2,1)S(1)} %reshape.75.source_ref, f32[4,128,256]{2,1,0:T(8,128)S(1)} %shard_map.109.spec_ref, bf16[2,256,128]{2,1,0:T(8,128)(2,1)S(1)} %copy-done.2, bf16[2,128,256]{2,1,0:T(8,128)(2,1)S(1)} %copy-done.5, bf16[2,256,256]{2,1,0:T(8,128)(2,1)S(1)} %copy-done.1, ...), custom_call_target="tpu_custom_call" | custom-call | tf_op jit(solution)/shard_map/pallas_call | solution.py:114
  149.6 0.1 reshape.79
  149.7 0.8 copy.76
  150.5 3.9 %all-to-all-start.5 = ((bf16[32,4,512]{2,1,0:T(4,128)(2,1)}), bf16[32,4,512]{2,1,0:T(4,128)(2,1)S(1)}, u32[]{:S(2)}, u32[]{:S(2)}) async-start(bf16[32,4,512]{2,1,0:T(4,128)(2,1)} %bitcast.38), calls=%async_computation.5 | async-start | bytes 262144 | tf_op jit(solution)/shard_map/all_to_all | solution.py:134
  154.3 0.1 dynamic_slice.10
  154.4 1.1 copy.62
  155.5 1.1 copy.64
  156.6 6.9 %all-to-all-done.5 = bf16[32,4,512]{2,1,0:T(4,128)(2,1)S(1)} async-done(((bf16[32,4,512]{2,1,0:T(4,128)(2,1)}), bf16[32,4,512]{2,1,0:T(4,128)(2,1)S(1)}, u32[]{:S(2)}, u32[]{:S(2)}) %all-to-all-start.5) | async-done | bytes 131104 | tf_op jit(solution)/shard_map/all_to_all | solution.py:134
  163.5 0.2 reshape.83
  163.6 0.1 fusion.5
  163.7 6.8 %all_to_all.47 = bf16[2,128,256]{2,1,0:T(8,128)(2,1)S(1)} all-to-all(bf16[2,128,256]{2,1,0:T(8,128)(2,1)S(1)} %fusion.5), channel_id=1, replica_groups={{0,8},{16,24},{32,40},{48,56},{64,72},{80,88},{96,104},{112,120},{128,1..., dimensions={0} | all-to-all | bytes 262144 | tf_op jit(solution)/shard_map/all_to_all | solution.py:134
  170.6 1.1 broadcast_in_dim.27
  171.7 3.7 %all-to-all-start.7 = ((bf16[8,256,256]{2,1,0:T(8,128)(2,1)}), bf16[8,256,256]{2,1,0:T(8,128)(2,1)S(1)}, u32[]{:S(2)}, u32[]{:S(2)}) async-start(bf16[8,256,256]{2,1,0:T(8,128)(2,1)} %broadcast_in_dim.27), calls=%async_computation.7 | async-start | bytes 2097152 | tf_op jit(solution)/shard_map/all_to_all | solution.py:134
  175.4 4.6 %copy.66 = bf16[8,64,4,512]{3,2,1,0:T(4,128)(2,1)} copy(bf16[8,64,4,512]{3,0,1,2:T(8,128)(2,1)} %bitcast.41) | data formatting | bytes 4194304 | tf_op jit(solution)/shard_map/transpose | solution.py:163
  180.0 4.0 %reshape.82 = bf16[2048,512]{1,0:T(8,128)(2,1)} reshape(bf16[8,64,4,512]{3,2,1,0:T(4,128)(2,1)} %copy.66) | data formatting | bytes 4194304 | tf_op jit(solution)/shard_map/reshape | solution.py:163
  184.0 18.2 %all-to-all-done.7 = bf16[8,256,256]{2,1,0:T(8,128)(2,1)S(1)} async-done(((bf16[8,256,256]{2,1,0:T(8,128)(2,1)}), bf16[8,256,256]{2,1,0:T(8,128)(2,1)S(1)}, u32[]{:S(2)}, u32[]{:S(2)}) %all-to-all-start.7) | async-done | bytes 1048608 | tf_op jit(solution)/shard_map/all_to_all | solution.py:134
  202.2 3.0 %convolution_convert_fusion = bf16[256,512]{1,0:T(8,128)(2,1)} fusion(bf16[2048,256]{1,0:T(8,128)(2,1)S(1)} %bitcast.42, bf16[2048,512]{1,0:T(8,128)(2,1)} %reshape.82), kind=kOutput, calls=%fused_computation | convolution fusion | flops 537001984 | bytes 3407872 | tf_op jit(solution)/shard_map/dot_general | solution.py:202
  (31 shorter events, 0.4 us)
Async XLA Ops:
  7.4 12.7 %copy-start = (bf16[256,4096]{1,0:T(8,128)(2,1)S(1)}, bf16[256,4096]{1,0:T(8,128)(2,1)}, u32[]{:S(2)}) copy-start(bf16[256,4096]{1,0:T(8,128)(2,1)} %param.16) | copy-start | bytes 6291460
  7.4 58.9 %all-gather.4.cloned.1.call-start = ((), (), s32[]{:S(2)}) async-start(), calls=%async_computation.9 | async-start | bytes 2359296 | tf_op jit(solution)/shard_map/all_gather | solution.py:141
  9.8 11.3 %all-to-all-start = ((bf16[2,64,384]{2,1,0:T(8,128)(2,1)}), bf16[2,64,384]{2,1,0:T(8,128)(2,1)S(1)}, u32[]{:S(2)}, u32[]{:S(2)}) async-start(bf16[2,64,384]{2,1,0:T(8,128)(2,1)} %reshape.74), calls=%async_computation | async-start | bytes 196608 | tf_op jit(solution)/shard_map/all_to_all | solution.py:134
  61.4 10.7 %copy-start.6 = (f32[256,256]{1,0:T(8,128)S(1)}, f32[256,256]{1,0:T(8,128)}, u32[]{:S(2)}) copy-start(f32[256,256]{1,0:T(8,128)} %param.14) | copy-start | bytes 786436
  61.4 39.1 %all-to-all-start.2 = ((bf16[4,1024,384]{2,1,0:T(8,128)(2,1)}), bf16[4,1024,384]{2,1,0:T(8,128)(2,1)}, u32[]{:S(2)}, u32[]{:S(2)}) async-start(bf16[4,1024,384]{2,1,0:T(8,128)(2,1)} %broadcast_in_dim.25), calls=%async_computation.2 | async-start | bytes 6291456 | tf_op jit(solution)/shard_map/all_to_all | solution.py:134
  66.2 109.3 %all-gather.6.cloned.1.call-start = ((), (), s32[]{:S(2)}) async-start(), calls=%async_computation.10 | async-start | bytes 2129920 | tf_op jit(solution)/shard_map/all_gather | solution.py:162
  66.2 47.8 %collective-permute-start = (bf16[256,4096]{1,0:T(8,128)(2,1)}, bf16[256,4096]{1,0:T(8,128)(2,1)}, u32[]{:S(2)}, u32[]{:S(2)}) collective-permute-start(bf16[256,4096]{1,0:T(8,128)(2,1)} %all-gather.4.cloned.1.call-done), channel_id=1, source_target_pairs={{0,8},{8,0},{16,24},{24,16},{32,40},{40,32},{48,56},{56,48},{64,72... | collective-permute-start | bytes 6291464 | tf_op jit(solution)/shard_map/ppermute | solution.py:139
  100.5 23.4 %all-to-all-start.4 = ((f32[64,4,256]{2,1,0:T(4,128)}), f32[64,4,256]{2,1,0:T(4,128)S(1)}, u32[]{:S(2)}, u32[]{:S(2)}) async-start(f32[64,4,256]{2,1,0:T(4,128)} %bitcast.12), calls=%async_computation.4 | async-start | bytes 524288 | tf_op jit(solution)/shard_map/all_to_all | solution.py:134
  114.0 7.2 %copy-start.7 = (f32[3,3,256]{2,1,0:T(4,128)S(1)}, f32[3,3,256]{2,1,0:T(4,128)}, u32[]{:S(2)}) copy-start(f32[3,3,256]{2,1,0:T(4,128)} %param.13) | copy-start | bytes 27652
  117.9 4.0 %collective-permute-start.1 = (f32[2,384]{1,0:T(2,128)S(1)}, f32[2,384]{1,0:T(2,128)S(1)}, u32[]{:S(2)}, u32[]{:S(2)}) collective-permute-start(f32[2,384]{1,0:T(2,128)S(1)} %slice.42), channel_id=1, source_target_pairs={{0,16},{8,24},{16,32},{24,40},{32,48},{40,56},{48,64},{56,72},{64,... | collective-permute-start | bytes 9224 | tf_op jit(solution)/shard_map/ppermute | solution.py:179
  122.2 13.0 %copy-start.1 = (bf16[2,256,256]{2,1,0:T(8,128)(2,1)S(1)}, bf16[2,256,256]{2,1,0:T(8,128)(2,1)}, u32[]{:S(2)}) copy-start(bf16[2,256,256]{2,1,0:T(8,128)(2,1)} %constant.37.clone.forward_ref) | copy-start | bytes 786436
  122.2 13.0 %copy-start.2 = (bf16[2,256,128]{2,1,0:T(8,128)(2,1)S(1)}, bf16[2,256,128]{2,1,0:T(8,128)(2,1)}, u32[]{:S(2)}) copy-start(bf16[2,256,128]{2,1,0:T(8,128)(2,1)} %constant.36.clone.columns_ref) | copy-start | bytes 393220
  122.2 13.0 %copy-start.3 = (f32[2,128,128]{2,1,0:T(8,128)S(1)}, f32[2,128,128]{2,1,0:T(8,128)}, u32[]{:S(2)}) copy-start(f32[2,128,128]{2,1,0:T(8,128)} %constant.38.clone.twist_ref) | copy-start | bytes 393220
  123.0 23.2 %copy-start.5 = (bf16[2,128,256]{2,1,0:T(8,128)(2,1)S(1)}, bf16[2,128,256]{2,1,0:T(8,128)(2,1)}, u32[]{:S(2)}) copy-start(bf16[2,128,256]{2,1,0:T(8,128)(2,1)} %constant.39.clone.rows_ref) | copy-start | bytes 393220
  123.9 21.3 %all-to-all-start.3 = ((bf16[32,4,512]{2,1,0:T(4,128)(2,1)}), bf16[32,4,512]{2,1,0:T(4,128)(2,1)}, u32[]{:S(2)}, u32[]{:S(2)}) async-start(bf16[32,4,512]{2,1,0:T(4,128)(2,1)} %convert_element_type.22), calls=%async_computation.3 | async-start | bytes 262144 | tf_op jit(solution)/shard_map/all_to_all | solution.py:134
  135.2 19.2 %copy-start.8 = (f32[256]{0:T(256)S(1)}, f32[256]{0:T(256)}, u32[]{:S(2)}) copy-start(f32[256]{0:T(256)} %param.15) | copy-start | bytes 3076
  146.2 1.0 copy-start.4
  150.5 13.0 %all-to-all-start.5 = ((bf16[32,4,512]{2,1,0:T(4,128)(2,1)}), bf16[32,4,512]{2,1,0:T(4,128)(2,1)S(1)}, u32[]{:S(2)}, u32[]{:S(2)}) async-start(bf16[32,4,512]{2,1,0:T(4,128)(2,1)} %bitcast.38), calls=%async_computation.5 | async-start | bytes 262144 | tf_op jit(solution)/shard_map/all_to_all | solution.py:134
  171.7 30.5 %all-to-all-start.7 = ((bf16[8,256,256]{2,1,0:T(8,128)(2,1)}), bf16[8,256,256]{2,1,0:T(8,128)(2,1)S(1)}, u32[]{:S(2)}, u32[]{:S(2)}) async-start(bf16[8,256,256]{2,1,0:T(8,128)(2,1)} %broadcast_in_dim.27), calls=%async_computation.7 | async-start | bytes 2097152 | tf_op jit(solution)/shard_map/all_to_all | solution.py:134
Sparse Core Ops, SparseCore 0:
  10.3 45.3 all-gather.3
Sparse Core Ops, SparseCore 1:
  73.7 83.1 all-gather.5
where the time goes:
time: 214 us; the launch traced here: 213 us
  waiting for transfers between devices  63.7 us (30%)
  starting transfers between devices  52.6 us (25%)
  blocking collectives  45 us (21%)
  local copies, waits for them, and re-layouts  21.1 us (10%)
  between operations  15.2 us (7%)
  matrix products  10.6 us (5%)
  Pallas kernels  3.17 us (1%)
    all_to_all x6, waiting for transfers between devices, exchange(): lax.all_to_all(value, axis, split_axis=0, concat_axis=0, tiled=True, axis...  62.2 us
    all_to_all x3, blocking collectives, exchange(): lax.all_to_all(value, axis, split_axis=0, concat_axis=0, tiled=True, axis...  45 us
    all_to_all x6, starting transfers between devices, exchange(): lax.all_to_all(value, axis, split_axis=0, concat_axis=0, tiled=True, axis...  43.5 us
    dot_general x2, matrix products, project(): return jnp.dot(value, weights, preferred_element_type=jnp.float32)  7.62 us
    ppermute x1, starting transfers between devices, swap(): return lax.ppermute(value, 'seq', [(i, i ^ 1) for i in range(seq_count)])  5.78 us
    transpose x1, local copies, waits for them, and re-layouts, body(): wanted = wanted.transpose(1, 0, 2, 3).reshape(-1, out_columns)  4.56 us
  transfers between devices with their start and end apart: 10, of which 6 were waited for; matrix products, arithmetic and copies ran while one was open for 14% of the time, Pallas kernels for 1%

commit v1 on v0

--- a/solution.py
+++ b/solution.py
@@ -119,16 +119,20 @@
 
 
 def body(groups, tokens, in_weight, short_taps, long_filter, skip, out_weight):
-    x_groups, z_groups, core_groups, chip_groups = groups
+    x_groups, zc_groups, chip_groups, column_groups = groups
     seq_count = lax.axis_size("seq")
     tp_count = lax.axis_size("tp")
     seq_index = lax.axis_index("seq")
+    tp_index = lax.axis_index("tp")
     core = seq_index % 2
     chips = seq_count // 2
     rows = tokens.shape[0]
+    chip_rows = 2 * rows
     depth = in_weight.shape[1]
-    half = in_weight.shape[2] // 2
+    width = in_weight.shape[2]
+    half = width // 2
     own = half // chips
+    features = tokens.shape[1]
 
     def exchange(value, axis, members):
         return lax.all_to_all(
@@ -138,67 +142,75 @@
     def swap(value):
         return lax.ppermute(value, "seq", [(i, i ^ 1) for i in range(seq_count)])
 
-    mine = lax.all_gather(tokens, "tp", axis=1, tiled=True)
+    members = len(zc_groups[0])
+    piece = out_weight.shape[0] // members
+    strip = lax.dynamic_slice_in_dim(out_weight, (seq_index % members) * piece, piece, 0)
+    strip = strip.reshape(piece, tp_count, features).transpose(1, 0, 2).reshape(-1, features)
+    mine = lax.all_gather(jnp.concatenate([tokens, strip], axis=0), "tp", axis=1, tiled=True)
+
+    weights = in_weight.reshape(3, depth, 2, half).transpose(2, 1, 0, 3)
+    weights = weights.reshape(1, 2, depth, 3 * half)
+    weights = exchange(
+        jnp.broadcast_to(weights, (members // 2, 2, depth, 3 * half)).reshape(-1, depth, 3 * half),
+        "seq",
+        zc_groups,
+    ).reshape(-1, 3 * half)
+    late_weights = lax.all_gather(
+        weights[:, width:], "seq", axis=0, tiled=True, axis_index_groups=x_groups
+    )
+    count = len(x_groups[0])
+    weights = jnp.broadcast_to(weights[None, :, :width], (count, weights.shape[0], width))
+    weights = exchange(weights, "seq", x_groups).reshape(-1, width)
+    mine, weights = lax.optimization_barrier((mine, weights))
     theirs = swap(mine)
-
-    weights = in_weight.reshape(3, depth, 2, half).transpose(2, 1, 0, 3).reshape(2, depth, 3 * half)
-    weights = exchange(weights, "seq", core_groups).reshape(1, 2 * depth, 3 * half)
-    for members in (z_groups, x_groups):
-        count = len(members[0])
-        weights = exchange(
-            jnp.broadcast_to(weights, (count,) + weights.shape[1:]), "seq", members
-        ).reshape(1, -1, 3 * half)
-    weights = weights[0]
 
     filter_in = long_filter.T.reshape(2, chips, own, rows).transpose(1, 0, 2, 3)
     filter_in = exchange(filter_in.reshape(seq_count, own, rows), "seq", None)
     filter_in = filter_in.transpose(1, 0, 2).reshape(own, SIDE, SIDE)
     spec = filter_spectrum(filter_in)
 
-    piece = out_weight.shape[0] // seq_count
-    out_columns = out_weight.shape[1] // tp_count
-    wanted = lax.dynamic_slice_in_dim(out_weight, seq_index * piece, piece, 0)
-    wanted = exchange(wanted.reshape(piece, tp_count, out_columns).transpose(1, 0, 2), "tp", None)
-    wanted = lax.all_gather(wanted, "seq", axis=0)
-    wanted = wanted.transpose(1, 0, 2, 3).reshape(-1, out_columns)
-
-    def project(value):
-        return jnp.dot(value, weights, preferred_element_type=jnp.float32)
-
-    projected_mine, projected_theirs = project(mine), project(theirs)
+    rim = short_taps.shape[0] - 1
     is_first = core == 0
-    projected = jnp.concatenate(
-        [
-            jnp.where(is_first, projected_mine, projected_theirs),
-            jnp.where(is_first, projected_theirs, projected_mine),
-        ],
-        axis=0,
-    )
-    chip_rows = 2 * rows
-    rim = short_taps.shape[0] - 1
-    before = lax.ppermute(
-        projected[chip_rows - rim :], "seq", [(i, i + 2) for i in range(seq_count - 2)]
-    )
-    extended = jnp.concatenate([before, projected], axis=0)
-    taps = lax.dynamic_slice_in_dim(short_taps, core * half, half, 2).reshape(rim + 1, 1, 3 * half)
-    mixed = sum(
-        taps[offset] * extended[rim - offset : rim - offset + chip_rows] for offset in range(rim + 1)
-    )
-    mixed = mixed.T.reshape(3, half, chip_rows)
-    source = mixed[1] * mixed[0]
-
-    blocks = exchange(source.astype(BF).reshape(chips, own, chip_rows), "seq", chip_groups)
+    own_taps = lax.dynamic_slice_in_dim(short_taps, core * half, half, 2)
+
+    def project(mine, table, taps):
+        first = jnp.dot(mine, table, preferred_element_type=jnp.float32)[:rows]
+        second = jnp.dot(theirs, table, preferred_element_type=jnp.float32)[:rows]
+        upper = jnp.where(is_first, first, second)
+        lower = jnp.where(is_first, second, first)
+        before = lax.ppermute(
+            lower[rows - rim :], "seq", [(i, i + 2) for i in range(seq_count - 2)]
+        )
+        extended = jnp.concatenate([before, upper, lower], axis=0)
+        return sum(
+            taps[offset] * extended[rim - offset : rim - offset + chip_rows]
+            for offset in range(rim + 1)
+        )
+
+    early = project(mine, weights, own_taps[:, :2].reshape(rim + 1, 1, width)).T
+    source = early[half:] * early[:half]
+
+    sent = source.astype(BF).reshape(chips, own, chip_rows)
+    sent, spec = lax.optimization_barrier((sent, spec))
+    later, _ = lax.optimization_barrier((mine, sent))
+    blocks = exchange(sent, "seq", chip_groups)
     blocks = blocks.transpose(1, 0, 2).reshape(own, SIDE, SIDE)
     result = long_convolution(blocks, spec)
     result = result.reshape(own, chips, chip_rows).transpose(1, 0, 2)
     long_conv = exchange(result, "seq", chip_groups).reshape(half, chip_rows)
 
+    strip = lax.dynamic_slice_in_dim(later, rows + tp_index * piece, piece, 0)
+    wanted = lax.all_gather(
+        strip.reshape(piece, tp_count, features), "seq", axis=0, axis_index_groups=zc_groups
+    )
+    wanted = wanted.transpose(2, 0, 1, 3).reshape(-1, features)
+
+    gate = project(later, late_weights, own_taps[:, 2].reshape(rim + 1, 1, half)).T
     own_skip = lax.dynamic_slice_in_dim(skip, core * half, half, 0)
-    gated = (mixed[2] * (long_conv.astype(jnp.float32) + own_skip[:, None] * source)).astype(BF)
-    gated = exchange(gated.reshape(half, 2, rows).transpose(1, 0, 2), "seq", core_groups)
-    gated = gated.reshape(1, 2 * half, rows)
-    gated = exchange(jnp.broadcast_to(gated, (tp_count,) + gated.shape[1:]), "tp", None)
-    gated = gated.reshape(-1, rows)
+    gated = (gate * (long_conv.astype(jnp.float32) + own_skip[:, None] * source)).astype(BF)
+    gated = gated.reshape(half, 2, rows).transpose(1, 0, 2)
+    gated = jnp.broadcast_to(gated, (tp_count,) + gated.shape).reshape(-1, half, rows)
+    gated = exchange(gated, ("seq", "tp"), column_groups).reshape(-1, rows)
     out = lax.dot_general(
         gated, wanted, (((0,), (0,)), ((), ())), preferred_element_type=jnp.float32
     )
@@ -206,16 +218,17 @@
 
 
 def solution(mesh):
-    width, depth = 4, 8
+    width, depth, tp = 4, 8, mesh.shape["tp"]
     place = lambda x, z, c: (x * depth + z) * 2 + c
+    chips = [(x, z) for x in range(width) for z in range(depth)]
     x_groups = [[place(x, z, c) for x in range(width)] for z in range(depth) for c in range(2)]
-    z_groups = [[place(x, z, c) for z in range(depth)] for x in range(width) for c in range(2)]
-    core_groups = [[place(x, z, c) for c in range(2)] for x in range(width) for z in range(depth)]
-    chip_groups = [
-        [place(x, z, c) for x in range(width) for z in range(depth)] for c in range(2)
+    zc_groups = [[place(x, z, c) for z in range(depth) for c in range(2)] for x in range(width)]
+    chip_groups = [[place(x, z, c) for x, z in chips] for c in range(2)]
+    column_groups = [
+        [place(x, z, c) * tp + y for y in range(tp) for c in range(2)] for x, z in chips
     ]
     return jax.shard_map(
-        functools.partial(body, (x_groups, z_groups, core_groups, chip_groups)),
+        functools.partial(body, (x_groups, zc_groups, chip_groups, column_groups)),
         mesh=mesh,
         in_specs=(
             P("seq", "tp"),

time: 214 us -> 195 us (0.911)
  waiting for transfers between devices: 63.7 us -> 32.4 us
  blocking collectives: 45 us -> 65.2 us
  starting transfers between devices: 52.6 us -> 41.3 us
  matrix products: 10.6 us -> 15.1 us
  local copies, waits for them, and re-layouts: 21.1 us -> 17.7 us
  other arithmetic: 1.19 us -> 4.05 us
    all_to_all x6 -> x4, waiting for transfers between devices: 62.2 us -> 20.1 us  [exchange(): lax.all_to_all(value, axis, split_axis=0, concat_axis=0, tiled=True, axis...]
    all_to_all x3 -> x2, blocking collectives: 45 us -> 65.2 us  [exchange(): lax.all_to_all(value, axis, split_axis=0, concat_axis=0, tiled=True, axis...]
    all_gather x2 -> x3, waiting for transfers between devices: 0.05 us -> 12.2 us  [the longest x1 8.63 us: body(): lax.all_gather(strip.reshape(piece, tp_count, features), 'seq', axis=0, a...]
    all_to_all x6 -> x4, starting transfers between devices: 43.5 us -> 32.3 us  [exchange(): lax.all_to_all(value, axis, split_axis=0, concat_axis=0, tiled=True, axis...]
    dot_general x2 -> x4, matrix products: 7.62 us -> 12.1 us  [the longest x2 6.28 us: project(): first = jnp.dot(mine, table, preferred_element_type=jnp.float32)[:rows]]
    transpose x1 -> x2, local copies, waits for them, and re-layouts: 4.56 us -> 0.16 us  [the longest x1 0.11 us: body(): gated = gated.reshape(half, 2, rows).transpose(1, 0, 2)]
    reshape x4 -> x3, local copies, waits for them, and re-layouts: 5.71 us -> 1.7 us  [the longest x2 1.01 us: body(): weights = in_weight.reshape(3, depth, 2, half).transpose(2, 1, 0, 3)]
    unnamed x18 -> x32, local copies, waits for them, and re-layouts: 0.99 us -> 4.83 us
  transfers between devices with their start and end apart: 10 -> 10, of which waited for: 6 -> 6; matrix products, arithmetic and copies ran while one was open for 14% -> 14% of each run, Pallas kernels for 1% -> 2%
where the time goes in v1:
time: 195 us; the launch traced here: 194 us
  blocking collectives  65.2 us (33%)
  starting transfers between devices  41.3 us (21%)
  waiting for transfers between devices  32.4 us (17%)
  local copies, waits for them, and re-layouts  17.7 us (9%)
  between operations  15.3 us (8%)
  matrix products  15.1 us (8%)
  other arithmetic  4.05 us (2%)
  Pallas kernels  3.16 us (2%)
    all_to_all x2, blocking collectives, exchange(): lax.all_to_all(value, axis, split_axis=0, concat_axis=0, tiled=True, axis...  65.2 us
    all_to_all x4, starting transfers between devices, exchange(): lax.all_to_all(value, axis, split_axis=0, concat_axis=0, tiled=True, axis...  32.3 us
    all_to_all x4, waiting for transfers between devices, exchange(): lax.all_to_all(value, axis, split_axis=0, concat_axis=0, tiled=True, axis...  20.1 us
    all_gather x1, waiting for transfers between devices, body(): lax.all_gather(strip.reshape(piece, tp_count, features), 'seq', axis=0, a...  8.63 us
    ppermute x2, starting transfers between devices, project(): lax.ppermute(lower[rows - rim:], 'seq', [(i, i + 2) for i in range(seq_co...  6.3 us
    dot_general x2, matrix products, project(): first = jnp.dot(mine, table, preferred_element_type=jnp.float32)[:rows]  6.28 us
    dot_general x2, matrix products, project(): second = jnp.dot(theirs, table, preferred_element_type=jnp.float32)[:rows]  5.84 us
    unnamed x32, local copies, waits for them, and re-layouts  4.83 us
  transfers between devices with their start and end apart: 10, of which 6 were waited for; matrix products, arithmetic and copies ran while one was open for 14% of the time, Pallas kernels for 2%

profile of v1, /device:TPU:1, one launch (start us, length us, event | category | flops | bytes accessed | tf_op | source)
XLA Modules:
  0.0 194.3 jit_solution(8806895590472339107)
XLA Ops:
  7.4 1.6 copy-done
  9.1 1.7 pad_maximum_fusion.1
  10.8 0.9 reshape.70
  12.0 0.1 broadcast_in_dim.18
  12.1 34.6 %all_to_all.30 = bf16[16,64,384]{2,1,0:T(8,128)(2,1)S(1)} all-to-all(bf16[16,64,384]{2,1,0:T(8,128)(2,1)S(1)} %bitcast.58), channel_id=1, replica_groups={{0,8,16,24,32,40,48,56,64,72,80,88,96,104,112,120},{128,136,144,152,160..., dimensions={0} | all-to-all | bytes 1572864 | tf_op jit(solution)/shard_map/all_to_all | solution.py:138
  46.7 0.1 broadcast_in_dim.19
  46.8 30.6 %all_to_all.31 = bf16[4,1024,256]{2,1,0:T(8,128)(2,1)} all-to-all(bf16[4,1024,256]{2,1,0:T(8,128)(2,1)S(1)} %broadcast_in_dim.19), channel_id=1, replica_groups={{0,128,256,384},{8,136,264,392},{16,144,272,400},{24,152,280,408},{32,1..., dimensions={0} | all-to-all | bytes 4194304 | tf_op jit(solution)/shard_map/all_to_all | solution.py:138
  77.5 2.6 %collective-permute-start = (bf16[384,4096]{1,0:T(8,128)(2,1)}, bf16[384,4096]{1,0:T(8,128)(2,1)}, u32[]{:S(2)}, u32[]{:S(2)}) collective-permute-start(bf16[384,4096]{1,0:T(8,128)(2,1)} %all-gather.4.cloned.1.call-done), channel_id=1, source_target_pairs={{0,8},{8,0},{16,24},{24,16},{32,40},{40,32},{48,56},{56,48},{64,72... | collective-permute-start | bytes 9437192 | tf_op jit(solution)/shard_map/ppermute | solution.py:143
  80.1 0.1 copy.37
  80.3 0.7 copy.38
  81.0 4.2 %all-to-all-start.2 = ((f32[64,4,256]{2,1,0:T(4,128)}), f32[64,4,256]{2,1,0:T(4,128)S(1)}, u32[]{:S(2)}, u32[]{:S(2)}) async-start(f32[64,4,256]{2,1,0:T(4,128)} %bitcast.13), calls=%async_computation.2 | async-start | bytes 524288 | tf_op jit(solution)/shard_map/all_to_all | solution.py:138
  85.2 0.7 slice.106
  86.1 3.1 %fusion.2 = f32[256,256]{1,0:T(8,128)S(1)} fusion(bf16[4096,256]{1,0:T(8,128)(2,1)} %bitcast.59, bf16[384,4096]{1,0:T(8,128)(2,1)} %all-gather.4.cloned.1.call-done), kind=kOutput, calls=%fused_computation.2 | convolution fusion | flops 536870912 | bytes 4456448 | tf_op jit(solution)/shard_map/dot_general | solution.py:177
  89.2 3.1 %broadcast_select_fusion.1 = (f32[256,256]{1,0:T(8,128)}, f32[256,256]{1,0:T(8,128)S(1)}) fusion(f32[256,256]{1,0:T(8,128)S(1)} %fusion.2, pred[]{:T(512)S(6)} %eq.6, bf16[4096,256]{1,0:T(8,128)(2,1)S(1)} %bitcast.60, bf16[384,4096]{1,0:T(8,128)(2,1)} %collective-permute-done), kind=kOutput, calls=%fused_computation.30 | convolution fusion | flops 537001984 | bytes 4980737 | tf_op jit(solution)/shard_map/dot_general | solution.py:178
  92.3 0.7 copy-done.9
  93.0 3.2 %collective-permute-start.1 = (f32[2,256]{1,0:T(2,128)S(1)}, f32[2,256]{1,0:T(2,128)S(1)}, u32[]{:S(2)}, u32[]{:S(2)}) collective-permute-start(f32[2,256]{1,0:T(2,128)S(1)} %slice.101), channel_id=1, source_target_pairs={{0,16},{8,24},{16,32},{24,40},{32,48},{40,56},{48,64},{56,72},{64,... | collective-permute-start | bytes 6152 | tf_op jit(solution)/shard_map/ppermute | solution.py:181
  96.2 0.7 fusion.18
  96.9 0.2 all-to-all-done.2
  97.2 0.7 shard_map.109.spec_ref
  98.0 1.1 pad_maximum_fusion
  99.1 0.1 fusion.9
  99.2 0.8 copy-done.6
  100.0 0.1 copy.36
  100.2 0.7 reshape.74
  100.9 0.9 constant_dynamic-slice_fusion.3
  101.8 0.7 copy.46
  102.5 10.0 %all-to-all-start.3 = ((bf16[32,4,512]{2,1,0:T(4,128)(2,1)}), bf16[32,4,512]{2,1,0:T(4,128)(2,1)S(1)}, u32[]{:S(2)}, u32[]{:S(2)}) async-start(bf16[32,4,512]{2,1,0:T(4,128)(2,1)} %reshape.74), calls=%async_computation.3 | async-start | bytes 262144 | tf_op jit(solution)/shard_map/all_to_all | solution.py:138
  112.6 3.6 %all-gather.6.cloned.1.call-done = bf16[4096,128]{1,0:T(8,128)(2,1)} async-done(((bf16[1024,128]{1,0:T(8,128)(2,1)}), bf16[4096,128]{1,0:T(8,128)(2,1)}) %all-gather.6.cloned.1.call-update) | async-done | bytes 1048592 | tf_op jit(solution)/shard_map/all_gather | solution.py:158
  116.1 3.2 %fusion = f32[256,128]{1,0:T(8,128)} fusion(bf16[4096,128]{1,0:T(8,128)(2,1)} %all-gather.6.cloned.1.call-done, bf16[384,4096]{1,0:T(8,128)(2,1)} %all-gather.4.cloned.1.call-done), kind=kOutput, calls=%fused_computation | convolution fusion | flops 268435456 | bytes 3276800 | tf_op jit(solution)/shard_map/dot_general | solution.py:177
  119.4 2.5 %all-to-all-done.3 = bf16[32,4,512]{2,1,0:T(4,128)(2,1)S(1)} async-done(((bf16[32,4,512]{2,1,0:T(4,128)(2,1)}), bf16[32,4,512]{2,1,0:T(4,128)(2,1)S(1)}, u32[]{:S(2)}, u32[]{:S(2)}) %all-to-all-start.3) | async-done | bytes 131104 | tf_op jit(solution)/shard_map/all_to_all | solution.py:138
  122.0 0.9 copy-done.4
  122.9 2.4 %shard_map.110 = bf16[4,128,128]{2,1,0:T(8,128)(2,1)S(1)} custom-call(bf16[4,128,128]{2,1,0:T(8,128)(2,1)S(1)} %reshape.78.source_ref, f32[4,128,256]{2,1,0:T(8,128)S(1)} %shard_map.109.spec_ref, bf16[2,256,128]{2,1,0:T(8,128)(2,1)S(1)} %copy-done.2, bf16[2,128,256]{2,1,0:T(8,128)(2,1)S(1)} %copy-done.5, bf16[2,256,256]{2,1,0:T(8,128)(2,1)S(1)} %copy-done.1, ...), custom_call_target="tpu_custom_call" | custom-call | tf_op jit(solution)/shard_map/pallas_call | solution.py:114
  125.4 0.7 copy.49
  126.2 7.8 %all-to-all-start.4 = ((bf16[32,4,512]{2,1,0:T(4,128)(2,1)}), bf16[32,4,512]{2,1,0:T(4,128)(2,1)S(1)}, u32[]{:S(2)}, u32[]{:S(2)}) async-start(bf16[32,4,512]{2,1,0:T(4,128)(2,1)} %bitcast.54), calls=%async_computation.4 | async-start | bytes 262144 | tf_op jit(solution)/shard_map/all_to_all | solution.py:138
  134.0 2.8 %broadcast_select_fusion.3 = (f32[256,128]{1,0:T(8,128)S(1)}, f32[256,128]{1,0:T(8,128)S(1)}) fusion(f32[256,128]{1,0:T(8,128)} %fusion, pred[]{:T(512)S(6)} %eq.6, bf16[4096,128]{1,0:T(8,128)(2,1)} %all-gather.6.cloned.1.call-done, bf16[384,4096]{1,0:T(8,128)(2,1)} %collective-permute-done), kind=kOutput, calls=%fused_computation.33 | convolution fusion | flops 268500992 | bytes 3538945 | tf_op jit(solution)/shard_map/dot_general | solution.py:178
  136.8 3.1 %collective-permute-start.2 = (f32[2,128]{1,0:T(2,128)S(1)}, f32[2,128]{1,0:T(2,128)S(1)}, u32[]{:S(2)}, u32[]{:S(2)}) collective-permute-start(f32[2,128]{1,0:T(2,128)S(1)} %slice.107), channel_id=1, source_target_pairs={{0,16},{8,24},{16,32},{24,40},{32,48},{40,56},{48,64},{56,72},{64,... | collective-permute-start | bytes 3080 | tf_op jit(solution)/shard_map/ppermute | solution.py:181
  139.9 0.8 fusion.20
  140.7 0.6 dynamic_slice.14
  141.4 1.8 all-to-all-done.4
  143.2 0.1 copy.42
  143.3 1.0 fusion.14
  144.4 0.1 copy.43
  144.5 1.1 broadcast_in_dim.20
  145.6 10.3 %all-to-all-start.5 = ((bf16[16,128,256]{2,1,0:T(8,128)(2,1)}), bf16[16,128,256]{2,1,0:T(8,128)(2,1)S(1)}, u32[]{:S(2)}, u32[]{:S(2)}) async-start(bf16[16,128,256]{2,1,0:T(8,128)(2,1)} %bitcast.22), calls=%async_computation.5 | async-start | bytes 2097152 | tf_op jit(solution)/shard_map/all_to_all | solution.py:138
  155.9 8.6 %all-gather.8.cloned.1.call-done = bf16[16,16,8,512]{3,2,1,0:T(8,128)(2,1)} async-done(((bf16[1,16,8,512]{3,2,1,0:T(8,128)(2,1)}), bf16[16,16,8,512]{3,2,1,0:T(8,128)(2,1)}) %all-gather.8.cloned.1.call-update) | async-done | bytes 2097168 | tf_op jit(solution)/shard_map/all_gather | solution.py:203
  164.5 3.6 %copy.44 = bf16[16,16,8,512]{3,1,0,2:T(8,128)(2,1)} copy(bf16[16,16,8,512]{3,2,1,0:T(8,128)(2,1)} %all-gather.8.cloned.1.call-done) | data formatting | bytes 4194304 | tf_op jit(solution)/shard_map/all_gather | solution.py:203
  168.2 15.7 %all-to-all-done.5 = bf16[16,128,256]{2,1,0:T(8,128)(2,1)S(1)} async-done(((bf16[16,128,256]{2,1,0:T(8,128)(2,1)}), bf16[16,128,256]{2,1,0:T(8,128)(2,1)S(1)}, u32[]{:S(2)}, u32[]{:S(2)}) %all-to-all-start.5) | async-done | bytes 1048608 | tf_op jit(solution)/shard_map/all_to_all | solution.py:138
  183.8 3.0 %convolution_convert_fusion = bf16[256,512]{1,0:T(8,128)(2,1)} fusion(bf16[2048,256]{1,0:T(8,128)(2,1)S(1)} %bitcast.62, bf16[2048,512]{1,0:T(8,128)(2,1)} %bitcast.61), kind=kOutput, calls=%fused_computation.8 | convolution fusion | flops 537001984 | bytes 3407872 | tf_op jit(solution)/shard_map/dot_general | solution.py:214
  (53 shorter events, 1.0 us)
Async XLA Ops:
  7.4 1.6 copy-start
  7.4 70.1 %all-gather.4.cloned.1.call-start = ((), (), s32[]{:S(2)}) async-start(), calls=%async_computation.6 | async-start | bytes 3538944 | tf_op jit(solution)/shard_map/all_gather | solution.py:149
  46.8 33.3 %copy-start.13 = (f32[256,256]{1,0:T(8,128)S(1)}, f32[256,256]{1,0:T(8,128)}, u32[]{:S(2)}) copy-start(f32[256,256]{1,0:T(8,128)} %param.14) | copy-start | bytes 786436
  77.5 11.7 %collective-permute-start = (bf16[384,4096]{1,0:T(8,128)(2,1)}, bf16[384,4096]{1,0:T(8,128)(2,1)}, u32[]{:S(2)}, u32[]{:S(2)}) collective-permute-start(bf16[384,4096]{1,0:T(8,128)(2,1)} %all-gather.4.cloned.1.call-done), channel_id=1, source_target_pairs={{0,8},{8,0},{16,24},{24,16},{32,40},{40,32},{48,56},{56,48},{64,72... | collective-permute-start | bytes 9437192 | tf_op jit(solution)/shard_map/ppermute | solution.py:143
  81.0 16.1 %all-to-all-start.2 = ((f32[64,4,256]{2,1,0:T(4,128)}), f32[64,4,256]{2,1,0:T(4,128)S(1)}, u32[]{:S(2)}, u32[]{:S(2)}) async-start(f32[64,4,256]{2,1,0:T(4,128)} %bitcast.13), calls=%async_computation.2 | async-start | bytes 524288 | tf_op jit(solution)/shard_map/all_to_all | solution.py:138
  85.2 31.0 %all-gather.6.cloned.1.call-start = ((), (), s32[]{:S(2)}) async-start(), calls=%async_computation.7 | async-start | bytes 1310720 | tf_op jit(solution)/shard_map/all_gather | solution.py:158
  86.0 78.5 %all-gather.8.cloned.1.call-start = ((), (), s32[]{:S(2)}) async-start(), calls=%async_computation.8 | async-start | bytes 2228224 | tf_op jit(solution)/shard_map/all_gather | solution.py:203
  86.0 3.1 %copy-start.8 = (bf16[4,1024,256]{2,1,0:T(8,128)(2,1)S(1)}, bf16[4,1024,256]{2,1,0:T(8,128)(2,1)}, u32[]{:S(2)}) copy-start(bf16[4,1024,256]{2,1,0:T(8,128)(2,1)} %all_to_all.31) | copy-start | bytes 6291460
  89.1 8.0 %copy-start.1 = (bf16[2,256,256]{2,1,0:T(8,128)(2,1)S(1)}, bf16[2,256,256]{2,1,0:T(8,128)(2,1)}, u32[]{:S(2)}) copy-start(bf16[2,256,256]{2,1,0:T(8,128)(2,1)} %constant.51.clone.forward_ref) | copy-start | bytes 786436
  89.2 8.0 %copy-start.2 = (bf16[2,256,128]{2,1,0:T(8,128)(2,1)S(1)}, bf16[2,256,128]{2,1,0:T(8,128)(2,1)}, u32[]{:S(2)}) copy-start(bf16[2,256,128]{2,1,0:T(8,128)(2,1)} %constant.50.clone.columns_ref) | copy-start | bytes 393220
  89.2 8.0 %copy-start.3 = (f32[2,128,128]{2,1,0:T(8,128)S(1)}, f32[2,128,128]{2,1,0:T(8,128)}, u32[]{:S(2)}) copy-start(f32[2,128,128]{2,1,0:T(8,128)} %constant.52.clone.twist_ref) | copy-start | bytes 393220
  92.3 0.7 copy-start.9
  93.0 5.0 %collective-permute-start.1 = (f32[2,256]{1,0:T(2,128)S(1)}, f32[2,256]{1,0:T(2,128)S(1)}, u32[]{:S(2)}, u32[]{:S(2)}) collective-permute-start(f32[2,256]{1,0:T(2,128)S(1)} %slice.101), channel_id=1, source_target_pairs={{0,16},{8,24},{16,32},{24,40},{32,48},{40,56},{48,64},{56,72},{64,... | collective-permute-start | bytes 6152 | tf_op jit(solution)/shard_map/ppermute | solution.py:181
  97.2 1.9 copy-start.10
  97.2 1.9 copy-start.11
  99.2 0.8 copy-start.6
  102.5 19.3 %all-to-all-start.3 = ((bf16[32,4,512]{2,1,0:T(4,128)(2,1)}), bf16[32,4,512]{2,1,0:T(4,128)(2,1)S(1)}, u32[]{:S(2)}, u32[]{:S(2)}) async-start(bf16[32,4,512]{2,1,0:T(4,128)(2,1)} %reshape.74), calls=%async_computation.3 | async-start | bytes 262144 | tf_op jit(solution)/shard_map/all_to_all | solution.py:138
  112.6 9.4 %copy-start.5 = (bf16[2,128,256]{2,1,0:T(8,128)(2,1)S(1)}, bf16[2,128,256]{2,1,0:T(8,128)(2,1)}, u32[]{:S(2)}) copy-start(bf16[2,128,256]{2,1,0:T(8,128)(2,1)} %constant.53.clone.rows_ref) | copy-start | bytes 393220
  121.9 1.0 copy-start.4
  126.2 17.0 %all-to-all-start.4 = ((bf16[32,4,512]{2,1,0:T(4,128)(2,1)}), bf16[32,4,512]{2,1,0:T(4,128)(2,1)S(1)}, u32[]{:S(2)}, u32[]{:S(2)}) async-start(bf16[32,4,512]{2,1,0:T(4,128)(2,1)} %bitcast.54), calls=%async_computation.4 | async-start | bytes 262144 | tf_op jit(solution)/shard_map/all_to_all | solution.py:138
  134.0 6.8 %copy-start.14 = (f32[256]{0:T(256)S(1)}, f32[256]{0:T(256)}, u32[]{:S(2)}) copy-start(f32[256]{0:T(256)} %param.15) | copy-start | bytes 3076
  134.0 9.4 %copy-start.7 = (f32[256,512]{0,1:T(8,128)S(1)}, f32[256,512]{0,1:T(8,128)}, u32[]{:S(2)}) copy-start(f32[256,512]{0,1:T(8,128)} %copy-done.6) | copy-start | bytes 1572868
  136.8 6.4 %copy-start.12 = (f32[256,128]{1,0:T(8,128)}, f32[256,128]{1,0:T(8,128)S(1)}, u32[]{:S(2)}) copy-start(f32[256,128]{1,0:T(8,128)S(1)} %get-tuple-element.17) | copy-start | bytes 393220
  136.8 4.6 %collective-permute-start.2 = (f32[2,128]{1,0:T(2,128)S(1)}, f32[2,128]{1,0:T(2,128)S(1)}, u32[]{:S(2)}, u32[]{:S(2)}) collective-permute-start(f32[2,128]{1,0:T(2,128)S(1)} %slice.107), channel_id=1, source_target_pairs={{0,16},{8,24},{16,32},{24,40},{32,48},{40,56},{48,64},{56,72},{64,... | collective-permute-start | bytes 3080 | tf_op jit(solution)/shard_map/ppermute | solution.py:181
  145.6 38.2 %all-to-all-start.5 = ((bf16[16,128,256]{2,1,0:T(8,128)(2,1)}), bf16[16,128,256]{2,1,0:T(8,128)(2,1)S(1)}, u32[]{:S(2)}, u32[]{:S(2)}) async-start(bf16[16,128,256]{2,1,0:T(8,128)(2,1)} %bitcast.22), calls=%async_computation.5 | async-start | bytes 2097152 | tf_op jit(solution)/shard_map/all_to_all | solution.py:138
Sparse Core Ops, SparseCore 0:
  11.0 52.3 all-gather.3
Sparse Core Ops, SparseCore 1:
  87.8 28.3 all-gather.5
  118.1 46.3 all-gather.7

commit v2 on v1

--- a/solution.py
+++ b/solution.py
@@ -118,6 +118,54 @@
     )(blocks, spec, columns, rows, forward, backward, twist)
 
 
+def product_kernel(side_ref, left_ref, right_ref, out_ref, total_ref):
+    step = pl.program_id(0)
+    table = right_ref[...].reshape(left_ref.shape[0], right_ref.shape[-1])
+    part = lax.dot_general(
+        left_ref[...], table, (((0,), (0,)), ((), ())), preferred_element_type=jnp.float32
+    )
+
+    @pl.when(step == 0)
+    def _():
+        total_ref[...] = part
+
+    @pl.when(step > 0)
+    def _():
+        total_ref[...] += part
+
+    @pl.when(step == pl.num_programs(0) - 1)
+    def _():
+        out_ref[...] = total_ref[...].astype(out_ref.dtype)
+
+
+def product(left, right, side, steps):
+    members, piece, columns = right.shape
+    piece //= 2
+    columns //= steps
+    block = members * piece
+    rows = left.shape[1]
+    return pl.pallas_call(
+        product_kernel,
+        grid_spec=pltpu.PrefetchScalarGridSpec(
+            num_scalar_prefetch=1,
+            grid=(steps,),
+            in_specs=[
+                pl.BlockSpec((block, rows), lambda k, side: (k, 0)),
+                pl.BlockSpec((members, piece, columns), lambda k, side: (0, side[0], k)),
+            ],
+            out_specs=pl.BlockSpec((rows, columns), lambda k, side: (0, 0)),
+            scratch_shapes=[pltpu.VMEM((rows, columns), jnp.float32)],
+        ),
+        out_shape=jax.ShapeDtypeStruct((rows, columns), BF),
+        cost_estimate=pl.CostEstimate(
+            flops=2 * rows * steps * block * columns,
+            bytes_accessed=2 * steps * block * (rows + columns),
+            transcendentals=0,
+        ),
+        compiler_params=pltpu.CompilerParams(vmem_limit_bytes=16 * 2**20),
+    )(side.reshape(1), left, right)
+
+
 def body(groups, tokens, in_weight, short_taps, long_filter, skip, out_weight):
     x_groups, zc_groups, chip_groups, column_groups = groups
     seq_count = lax.axis_size("seq")
@@ -167,8 +215,6 @@
     filter_in = long_filter.T.reshape(2, chips, own, rows).transpose(1, 0, 2, 3)
     filter_in = exchange(filter_in.reshape(seq_count, own, rows), "seq", None)
     filter_in = filter_in.transpose(1, 0, 2).reshape(own, SIDE, SIDE)
-    spec = filter_spectrum(filter_in)
-
     rim = short_taps.shape[0] - 1
     is_first = core == 0
     own_taps = lax.dynamic_slice_in_dim(short_taps, core * half, half, 2)
@@ -191,30 +237,37 @@
     source = early[half:] * early[:half]
 
     sent = source.astype(BF).reshape(chips, own, chip_rows)
-    sent, spec = lax.optimization_barrier((sent, spec))
+    sent, filter_in = lax.optimization_barrier((sent, filter_in))
     later, _ = lax.optimization_barrier((mine, sent))
     blocks = exchange(sent, "seq", chip_groups)
     blocks = blocks.transpose(1, 0, 2).reshape(own, SIDE, SIDE)
-    result = long_convolution(blocks, spec)
+    result = long_convolution(blocks, filter_spectrum(filter_in))
     result = result.reshape(own, chips, chip_rows).transpose(1, 0, 2)
     long_conv = exchange(result, "seq", chip_groups).reshape(half, chip_rows)
 
-    strip = lax.dynamic_slice_in_dim(later, rows + tp_index * piece, piece, 0)
+    pair_piece = 2 * piece
+    strip = lax.dynamic_slice_in_dim(
+        later, rows + (tp_index // 2) * pair_piece, pair_piece, 0
+    )
     wanted = lax.all_gather(
-        strip.reshape(piece, tp_count, features), "seq", axis=0, axis_index_groups=zc_groups
-    )
-    wanted = wanted.transpose(2, 0, 1, 3).reshape(-1, features)
+        strip, "seq", axis=0, axis_index_groups=zc_groups
+    )
 
     gate = project(later, late_weights, own_taps[:, 2].reshape(rim + 1, 1, half)).T
     own_skip = lax.dynamic_slice_in_dim(skip, core * half, half, 0)
     gated = (gate * (long_conv.astype(jnp.float32) + own_skip[:, None] * source)).astype(BF)
-    gated = gated.reshape(half, 2, rows).transpose(1, 0, 2)
-    gated = jnp.broadcast_to(gated, (tp_count,) + gated.shape).reshape(-1, half, rows)
-    gated = exchange(gated, ("seq", "tp"), column_groups).reshape(-1, rows)
-    out = lax.dot_general(
-        gated, wanted, (((0,), (0,)), ((), ())), preferred_element_type=jnp.float32
-    )
-    return out.astype(BF)
+    quarter = rows // 2
+    gated = gated.reshape(half, 2, 2, quarter).transpose(2, 1, 0, 3)
+    gated = jnp.broadcast_to(gated, (tp_count // 2,) + gated.shape).reshape(-1, half, quarter)
+    gated = exchange(gated, ("seq", "tp"), column_groups).reshape(-1, quarter)
+    side = tp_index % 2
+    given = product(gated, wanted, 1 - side, tp_count)
+    given = lax.ppermute(given, "tp", [(i, i ^ 1) for i in range(tp_count)])
+    kept = product(gated, wanted, side, tp_count)
+    is_even = side == 0
+    return jnp.concatenate(
+        [jnp.where(is_even, kept, given), jnp.where(is_even, given, kept)], axis=0
+    )
 
 
 def solution(mesh):

time: 195 us -> 195 us (level)
  waiting for transfers between devices: 32.4 us -> 27 us
  Pallas kernels: 3.16 us -> 7.5 us
  matrix products: 15.1 us -> 11.3 us
  local copies, waits for them, and re-layouts: 17.7 us -> 20 us
    all_gather x1, waiting for transfers between devices: 8.63 us -> 0.01 us  [body(): wanted = lax.all_gather(strip, 'seq', axis=0, axis_index_groups=zc_groups)]
    pallas_call x0 -> x2, Pallas kernels: none -> 4.34 us  [product(): pl.pallas_call(product_kernel, grid_spec=pltpu.PrefetchScalarGridSpec(num...]
    all_gather x1 -> x0, local copies, waits for them, and re-layouts: 3.63 us -> none  [body(): lax.all_gather(strip.reshape(piece, tp_count, features), 'seq', axis=0, a...]
    all_to_all x4, waiting for transfers between devices: 20.1 us -> 23.5 us  [exchange(): lax.all_to_all(value, axis, split_axis=0, concat_axis=0, tiled=True, axis...]
    dot_general x1 -> x0, matrix products: 3.02 us -> none  [body(): lax.dot_general(gated, wanted, (((0,), (0,)), ((), ())), preferred_elemen...]
    unnamed x32 -> x33, local copies, waits for them, and re-layouts: 4.83 us -> 7.01 us
  transfers between devices with their start and end apart: 10 -> 11, of which waited for: 6 -> 6; matrix products, arithmetic and copies ran while one was open for 14% -> 14% of each run, Pallas kernels for 2% -> 3%
where the time goes in v2:
time: 195 us; the launch traced here: 194 us
  blocking collectives  65.2 us (33%)
  starting transfers between devices  42.9 us (22%)
  waiting for transfers between devices  27 us (14%)
  local copies, waits for them, and re-layouts  20 us (10%)
  between operations  15.3 us (8%)
  matrix products  11.3 us (6%)
  Pallas kernels  7.5 us (4%)
  other arithmetic  4.82 us (2%)
    all_to_all x2, blocking collectives, exchange(): lax.all_to_all(value, axis, split_axis=0, concat_axis=0, tiled=True, axis...  65.2 us
    all_to_all x4, starting transfers between devices, exchange(): lax.all_to_all(value, axis, split_axis=0, concat_axis=0, tiled=True, axis...  32 us
    all_to_all x4, waiting for transfers between devices, exchange(): lax.all_to_all(value, axis, split_axis=0, concat_axis=0, tiled=True, axis...  23.5 us
    unnamed x33, local copies, waits for them, and re-layouts  7.01 us
    ppermute x2, starting transfers between devices, project(): lax.ppermute(lower[rows - rim:], 'seq', [(i, i + 2) for i in range(seq_co...  6.32 us
    dot_general x2, matrix products, project(): first = jnp.dot(mine, table, preferred_element_type=jnp.float32)[:rows]  6.28 us
    dot_general x2, matrix products, project(): second = jnp.dot(theirs, table, preferred_element_type=jnp.float32)[:rows]  5 us
    pallas_call x2, Pallas kernels, product(): pl.pallas_call(product_kernel, grid_spec=pltpu.PrefetchScalarGridSpec(num...  4.34 us
  transfers between devices with their start and end apart: 11, of which 6 were waited for; matrix products, arithmetic and copies ran while one was open for 14% of the time, Pallas kernels for 3%

profile of v2, /device:TPU:1, one launch (start us, length us, event | category | flops | bytes accessed | tf_op | source)
XLA Modules:
  0.0 194.0 jit_solution(7241613995469837663)
XLA Ops:
  7.4 1.6 copy-done
  9.1 1.7 pad_maximum_fusion.1
  10.8 0.9 reshape.74
  12.0 34.6 %all_to_all.30 = bf16[16,64,384]{2,1,0:T(8,128)(2,1)S(1)} all-to-all(bf16[16,64,384]{2,1,0:T(8,128)(2,1)S(1)} %bitcast.57), channel_id=1, replica_groups={{0,8,16,24,32,40,48,56,64,72,80,88,96,104,112,120},{128,136,144,152,160..., dimensions={0} | all-to-all | bytes 1572864 | tf_op jit(solution)/shard_map/all_to_all | solution.py:186
  46.7 0.1 broadcast_in_dim.19
  46.8 30.6 %all_to_all.31 = bf16[4,1024,256]{2,1,0:T(8,128)(2,1)} all-to-all(bf16[4,1024,256]{2,1,0:T(8,128)(2,1)S(1)} %broadcast_in_dim.19), channel_id=1, replica_groups={{0,128,256,384},{8,136,264,392},{16,144,272,400},{24,152,280,408},{32,1..., dimensions={0} | all-to-all | bytes 4194304 | tf_op jit(solution)/shard_map/all_to_all | solution.py:186
  77.4 2.6 %collective-permute-start = (bf16[384,4096]{1,0:T(8,128)(2,1)}, bf16[384,4096]{1,0:T(8,128)(2,1)}, u32[]{:S(2)}, u32[]{:S(2)}) collective-permute-start(bf16[384,4096]{1,0:T(8,128)(2,1)} %all-gather.5.cloned.1.call-done), channel_id=1, source_target_pairs={{0,8},{8,0},{16,24},{24,16},{32,40},{40,32},{48,56},{56,48},{64,72... | collective-permute-start | bytes 9437192 | tf_op jit(solution)/shard_map/ppermute | solution.py:191
  80.1 0.1 copy.26
  80.3 0.7 copy.27
  81.0 4.2 %all-to-all-start.2 = ((f32[64,4,256]{2,1,0:T(4,128)}), f32[64,4,256]{2,1,0:T(4,128)S(1)}, u32[]{:S(2)}, u32[]{:S(2)}) async-start(f32[64,4,256]{2,1,0:T(4,128)} %bitcast.14), calls=%async_computation.2 | async-start | bytes 524288 | tf_op jit(solution)/shard_map/all_to_all | solution.py:186
  85.3 0.7 slice.106
  86.1 3.1 %fusion.2 = f32[256,256]{1,0:T(8,128)S(1)} fusion(bf16[4096,256]{1,0:T(8,128)(2,1)} %bitcast.58, bf16[384,4096]{1,0:T(8,128)(2,1)} %all-gather.5.cloned.1.call-done), kind=kOutput, calls=%fused_computation.2 | convolution fusion | flops 536870912 | bytes 4456448 | tf_op jit(solution)/shard_map/dot_general | solution.py:223
  89.2 2.3 %broadcast_select_fusion.1 = (f32[256,256]{1,0:T(8,128)S(1)}, f32[256,256]{1,0:T(8,128)S(1)}) fusion(f32[256,256]{1,0:T(8,128)S(1)} %fusion.2, pred[]{:T(512)S(6)} %eq.11, bf16[4096,256]{1,0:T(8,128)(2,1)S(1)} %bitcast.59, bf16[384,4096]{1,0:T(8,128)(2,1)} %collective-permute-done), kind=kOutput, calls=%fused_computation.30 | convolution fusion | flops 537001984 | bytes 4980737 | tf_op jit(solution)/shard_map/dot_general | solution.py:224
  91.5 3.2 %collective-permute-start.1 = (f32[2,256]{1,0:T(2,128)S(1)}, f32[2,256]{1,0:T(2,128)S(1)}, u32[]{:S(2)}, u32[]{:S(2)}) collective-permute-start(f32[2,256]{1,0:T(2,128)S(1)} %slice.101), channel_id=1, source_target_pairs={{0,16},{8,24},{16,32},{24,40},{32,48},{40,56},{48,64},{56,72},{64,... | collective-permute-start | bytes 6152 | tf_op jit(solution)/shard_map/ppermute | solution.py:227
  94.7 0.7 fusion.18
  95.4 1.7 all-to-all-done.2
  97.3 1.2 fusion.9
  98.6 0.8 copy.25
  99.4 1.6 reshape.78
  100.9 1.7 constant_dynamic-slice_fusion.3
  102.7 9.4 %all-to-all-start.3 = ((bf16[32,4,512]{2,1,0:T(4,128)(2,1)}), bf16[32,4,512]{2,1,0:T(4,128)(2,1)S(1)}, u32[]{:S(2)}, u32[]{:S(2)}) async-start(bf16[32,4,512]{2,1,0:T(4,128)(2,1)} %reshape.78), calls=%async_computation.3 | async-start | bytes 262144 | tf_op jit(solution)/shard_map/all_to_all | solution.py:186
  112.1 0.7 shard_map.109.spec_ref
  112.8 3.3 %all-gather.7.cloned.1.call-done = bf16[4096,128]{1,0:T(8,128)(2,1)} async-done(((bf16[1024,128]{1,0:T(8,128)(2,1)}), bf16[4096,128]{1,0:T(8,128)(2,1)}) %all-gather.7.cloned.1.call-update) | async-done | bytes 1048592 | tf_op jit(solution)/shard_map/all_gather | solution.py:206
  116.2 3.2 %fusion = f32[256,128]{1,0:T(8,128)} fusion(bf16[4096,128]{1,0:T(8,128)(2,1)} %all-gather.7.cloned.1.call-done, bf16[384,4096]{1,0:T(8,128)(2,1)} %all-gather.5.cloned.1.call-done), kind=kOutput, calls=%fused_computation | convolution fusion | flops 268435456 | bytes 3276800 | tf_op jit(solution)/shard_map/dot_general | solution.py:223
  119.4 1.9 all-to-all-done.3
  121.3 0.7 copy.29
  122.0 1.0 reshape.82.source_ref
  123.0 0.9 copy-done.6
  123.9 2.4 %shard_map.110 = bf16[4,128,128]{2,1,0:T(8,128)(2,1)S(1)} custom-call(bf16[4,128,128]{2,1,0:T(8,128)(2,1)S(1)} %reshape.82.source_ref, f32[4,128,256]{2,1,0:T(8,128)S(1)} %shard_map.109.spec_ref, bf16[2,256,128]{2,1,0:T(8,128)(2,1)S(1)} %copy-done.4, bf16[2,128,256]{2,1,0:T(8,128)(2,1)S(1)} %copy-done.7, bf16[2,256,256]{2,1,0:T(8,128)(2,1)S(1)} %copy-done.3, ...), custom_call_target="tpu_custom_call" | custom-call | tf_op jit(solution)/shard_map/pallas_call | solution.py:114
  126.5 0.8 copy.36
  127.2 8.2 %all-to-all-start.4 = ((bf16[32,4,512]{2,1,0:T(4,128)(2,1)}), bf16[32,4,512]{2,1,0:T(4,128)(2,1)S(1)}, u32[]{:S(2)}, u32[]{:S(2)}) async-start(bf16[32,4,512]{2,1,0:T(4,128)(2,1)} %bitcast.49), calls=%async_computation.4 | async-start | bytes 262144 | tf_op jit(solution)/shard_map/all_to_all | solution.py:186
  135.4 2.7 %broadcast_select_fusion.5 = (f32[256,128]{1,0:T(8,128)S(1)}, f32[256,128]{1,0:T(8,128)S(1)}) fusion(f32[256,128]{1,0:T(8,128)} %fusion, pred[]{:T(512)S(6)} %eq.11, bf16[4096,128]{1,0:T(8,128)(2,1)} %all-gather.7.cloned.1.call-done, bf16[384,4096]{1,0:T(8,128)(2,1)} %collective-permute-done), kind=kOutput, calls=%fused_computation.35 | convolution fusion | flops 268500992 | bytes 3538945 | tf_op jit(solution)/shard_map/dot_general | solution.py:224
  138.1 3.1 %collective-permute-start.2 = (f32[2,128]{1,0:T(2,128)S(1)}, f32[2,128]{1,0:T(2,128)S(1)}, u32[]{:S(2)}, u32[]{:S(2)}) collective-permute-start(f32[2,128]{1,0:T(2,128)S(1)} %slice.107), channel_id=1, source_target_pairs={{0,16},{8,24},{16,32},{24,40},{32,48},{40,56},{48,64},{56,72},{64,... | collective-permute-start | bytes 3080 | tf_op jit(solution)/shard_map/ppermute | solution.py:227
  141.3 0.8 fusion.20
  142.1 0.6 dynamic_slice.14
  142.7 2.6 %all-to-all-done.4 = bf16[32,4,512]{2,1,0:T(4,128)(2,1)S(1)} async-done(((bf16[32,4,512]{2,1,0:T(4,128)(2,1)}), bf16[32,4,512]{2,1,0:T(4,128)(2,1)S(1)}, u32[]{:S(2)}, u32[]{:S(2)}) %all-to-all-start.4) | async-done | bytes 131104 | tf_op jit(solution)/shard_map/all_to_all | solution.py:186
  145.3 0.1 copy.31
  145.5 1.0 fusion.14
  146.5 0.1 copy.32
  146.6 0.9 broadcast_in_dim.20
  147.5 10.3 %all-to-all-start.5 = ((bf16[16,128,128]{2,1,0:T(8,128)(2,1)}), bf16[16,128,128]{2,1,0:T(8,128)(2,1)S(1)}, u32[]{:S(2)}, u32[]{:S(2)}) async-start(bf16[16,128,128]{2,1,0:T(8,128)(2,1)} %bitcast.23), calls=%async_computation.5 | async-start | bytes 1048576 | tf_op jit(solution)/shard_map/all_to_all | solution.py:186
  157.8 17.3 %all-to-all-done.5 = bf16[16,128,128]{2,1,0:T(8,128)(2,1)S(1)} async-done(((bf16[16,128,128]{2,1,0:T(8,128)(2,1)}), bf16[16,128,128]{2,1,0:T(8,128)(2,1)S(1)}, u32[]{:S(2)}, u32[]{:S(2)}) %all-to-all-start.5) | async-done | bytes 524320 | tf_op jit(solution)/shard_map/all_to_all | solution.py:186
  175.1 2.2 %copy-done.1 = bf16[512,4096]{1,0:T(8,128)(2,1)S(1)} copy-done((bf16[512,4096]{1,0:T(8,128)(2,1)S(1)}, bf16[512,4096]{1,0:T(8,128)(2,1)}, u32[]{:S(2)}) %copy-start.1) | copy-done | bytes 4194328
  177.3 2.2 %shard_map.112 = bf16[128,512]{1,0:T(8,128)(2,1)S(1)} custom-call(s32[1]{0:T(128)} %bitcast.26.side_ref, bf16[2048,128]{1,0:T(8,128)(2,1)S(1)} %bitcast.53, bf16[16,32,4096]{2,1,0:T(8,128)(2,1)S(1)} %bitcast.51), custom_call_target="tpu_custom_call" | custom-call | flops 268435456 | bytes 2621440 | tf_op jit(solution)/shard_map/pallas_call | solution.py:147
  179.5 1.9 collective-permute-start.3
  181.4 2.2 %copy-done.2 = bf16[512,4096]{1,0:T(8,128)(2,1)S(1)} copy-done((bf16[512,4096]{1,0:T(8,128)(2,1)S(1)}, bf16[512,4096]{1,0:T(8,128)(2,1)}, u32[]{:S(2)}) %copy-start.2) | copy-done | bytes 4194328
  183.6 2.2 %shard_map.111 = bf16[128,512]{1,0:T(8,128)(2,1)S(1)} custom-call(s32[1]{0:T(128)} %bitcast.side_ref, bf16[2048,128]{1,0:T(8,128)(2,1)S(1)} %bitcast.54, bf16[16,32,4096]{2,1,0:T(8,128)(2,1)S(1)} %bitcast.52), custom_call_target="tpu_custom_call" | custom-call | flops 268435456 | bytes 2621440 | tf_op jit(solution)/shard_map/pallas_call | solution.py:147
  185.9 0.7 pad_maximum_fusion.3
  (58 shorter events, 1.1 us)
Async XLA Ops:
  7.4 1.6 copy-start
  7.4 70.1 %all-gather.5.cloned.1.call-start = ((), (), s32[]{:S(2)}) async-start(), calls=%async_computation.6 | async-start | bytes 3538944 | tf_op jit(solution)/shard_map/all_gather | solution.py:197
  46.8 33.3 %copy-start.14 = (f32[256,256]{1,0:T(8,128)S(1)}, f32[256,256]{1,0:T(8,128)}, u32[]{:S(2)}) copy-start(f32[256,256]{1,0:T(8,128)} %param.14) | copy-start | bytes 786436
  77.4 11.7 %collective-permute-start = (bf16[384,4096]{1,0:T(8,128)(2,1)}, bf16[384,4096]{1,0:T(8,128)(2,1)}, u32[]{:S(2)}, u32[]{:S(2)}) collective-permute-start(bf16[384,4096]{1,0:T(8,128)(2,1)} %all-gather.5.cloned.1.call-done), channel_id=1, source_target_pairs={{0,8},{8,0},{16,24},{24,16},{32,40},{40,32},{48,56},{56,48},{64,72... | collective-permute-start | bytes 9437192 | tf_op jit(solution)/shard_map/ppermute | solution.py:191
  81.0 16.1 %all-to-all-start.2 = ((f32[64,4,256]{2,1,0:T(4,128)}), f32[64,4,256]{2,1,0:T(4,128)S(1)}, u32[]{:S(2)}, u32[]{:S(2)}) async-start(f32[64,4,256]{2,1,0:T(4,128)} %bitcast.14), calls=%async_computation.2 | async-start | bytes 524288 | tf_op jit(solution)/shard_map/all_to_all | solution.py:186
  85.2 31.0 %all-gather.7.cloned.1.call-start = ((), (), s32[]{:S(2)}) async-start(), calls=%async_computation.7 | async-start | bytes 1310720 | tf_op jit(solution)/shard_map/all_gather | solution.py:206
  86.0 89.1 %all-gather.9.cloned.1.call-start = ((), (), s32[]{:S(2)}) async-start(), calls=%async_computation.8 | async-start | bytes 4456448 | tf_op jit(solution)/shard_map/all_gather | solution.py:252
  86.1 3.1 %copy-start.10 = (bf16[4,1024,256]{2,1,0:T(8,128)(2,1)S(1)}, bf16[4,1024,256]{2,1,0:T(8,128)(2,1)}, u32[]{:S(2)}) copy-start(bf16[4,1024,256]{2,1,0:T(8,128)(2,1)} %all_to_all.31) | copy-start | bytes 6291460
  91.5 5.7 %copy-start.11 = (f32[256,256]{1,0:T(8,128)}, f32[256,256]{1,0:T(8,128)S(1)}, u32[]{:S(2)}) copy-start(f32[256,256]{1,0:T(8,128)S(1)} %get-tuple-element.16) | copy-start | bytes 786436
  91.5 5.7 %copy-start.12 = (f32[256,256]{1,0:T(8,128)}, f32[256,256]{1,0:T(8,128)S(1)}, u32[]{:S(2)}) copy-start(f32[256,256]{1,0:T(8,128)S(1)} %get-tuple-element.15) | copy-start | bytes 786436
  91.5 5.7 %collective-permute-start.1 = (f32[2,256]{1,0:T(2,128)S(1)}, f32[2,256]{1,0:T(2,128)S(1)}, u32[]{:S(2)}, u32[]{:S(2)}) collective-permute-start(f32[2,256]{1,0:T(2,128)S(1)} %slice.101), channel_id=1, source_target_pairs={{0,16},{8,24},{16,32},{24,40},{32,48},{40,56},{48,64},{56,72},{64,... | collective-permute-start | bytes 6152 | tf_op jit(solution)/shard_map/ppermute | solution.py:227
  97.3 14.8 %copy-start.3 = (bf16[2,256,256]{2,1,0:T(8,128)(2,1)S(1)}, bf16[2,256,256]{2,1,0:T(8,128)(2,1)}, u32[]{:S(2)}) copy-start(bf16[2,256,256]{2,1,0:T(8,128)(2,1)} %constant.69.clone.forward_ref) | copy-start | bytes 786436
  97.3 14.8 %copy-start.4 = (bf16[2,256,128]{2,1,0:T(8,128)(2,1)S(1)}, bf16[2,256,128]{2,1,0:T(8,128)(2,1)}, u32[]{:S(2)}) copy-start(bf16[2,256,128]{2,1,0:T(8,128)(2,1)} %constant.68.clone.columns_ref) | copy-start | bytes 393220
  97.3 14.8 %copy-start.5 = (f32[2,128,128]{2,1,0:T(8,128)S(1)}, f32[2,128,128]{2,1,0:T(8,128)}, u32[]{:S(2)}) copy-start(f32[2,128,128]{2,1,0:T(8,128)} %constant.70.clone.twist_ref) | copy-start | bytes 393220
  98.5 4.1 %copy-start.8 = (f32[256,512]{0,1:T(8,128)}, f32[256,512]{0,1:T(8,128)S(1)}, u32[]{:S(2)}) copy-start(f32[256,512]{0,1:T(8,128)S(1)} %fusion.9) | copy-start | bytes 1572868
  102.7 18.6 %all-to-all-start.3 = ((bf16[32,4,512]{2,1,0:T(4,128)(2,1)}), bf16[32,4,512]{2,1,0:T(4,128)(2,1)S(1)}, u32[]{:S(2)}, u32[]{:S(2)}) async-start(bf16[32,4,512]{2,1,0:T(4,128)(2,1)} %reshape.78), calls=%async_computation.3 | async-start | bytes 262144 | tf_op jit(solution)/shard_map/all_to_all | solution.py:186
  112.8 10.1 %copy-start.7 = (bf16[2,128,256]{2,1,0:T(8,128)(2,1)S(1)}, bf16[2,128,256]{2,1,0:T(8,128)(2,1)}, u32[]{:S(2)}) copy-start(bf16[2,128,256]{2,1,0:T(8,128)(2,1)} %constant.71.clone.rows_ref) | copy-start | bytes 393220
  123.0 1.0 copy-start.6
  127.2 18.1 %all-to-all-start.4 = ((bf16[32,4,512]{2,1,0:T(4,128)(2,1)}), bf16[32,4,512]{2,1,0:T(4,128)(2,1)S(1)}, u32[]{:S(2)}, u32[]{:S(2)}) async-start(bf16[32,4,512]{2,1,0:T(4,128)(2,1)} %bitcast.49), calls=%async_computation.4 | async-start | bytes 262144 | tf_op jit(solution)/shard_map/all_to_all | solution.py:186
  135.4 6.7 %copy-start.15 = (f32[256]{0:T(256)S(1)}, f32[256]{0:T(256)}, u32[]{:S(2)}) copy-start(f32[256]{0:T(256)} %param.15) | copy-start | bytes 3076
  135.4 10.0 %copy-start.9 = (f32[256,512]{0,1:T(8,128)S(1)}, f32[256,512]{0,1:T(8,128)}, u32[]{:S(2)}) copy-start(f32[256,512]{0,1:T(8,128)} %copy-done.8) | copy-start | bytes 1572868
  138.1 7.2 %copy-start.13 = (f32[256,128]{1,0:T(8,128)}, f32[256,128]{1,0:T(8,128)S(1)}, u32[]{:S(2)}) copy-start(f32[256,128]{1,0:T(8,128)S(1)} %get-tuple-element.19) | copy-start | bytes 393220
  138.1 4.5 %collective-permute-start.2 = (f32[2,128]{1,0:T(2,128)S(1)}, f32[2,128]{1,0:T(2,128)S(1)}, u32[]{:S(2)}, u32[]{:S(2)}) collective-permute-start(f32[2,128]{1,0:T(2,128)S(1)} %slice.107), channel_id=1, source_target_pairs={{0,16},{8,24},{16,32},{24,40},{32,48},{40,56},{48,64},{56,72},{64,... | collective-permute-start | bytes 3080 | tf_op jit(solution)/shard_map/ppermute | solution.py:227
  147.5 27.6 %all-to-all-start.5 = ((bf16[16,128,128]{2,1,0:T(8,128)(2,1)}), bf16[16,128,128]{2,1,0:T(8,128)(2,1)S(1)}, u32[]{:S(2)}, u32[]{:S(2)}) async-start(bf16[16,128,128]{2,1,0:T(8,128)(2,1)} %bitcast.23), calls=%async_computation.5 | async-start | bytes 1048576 | tf_op jit(solution)/shard_map/all_to_all | solution.py:186
  175.1 2.2 %copy-start.1 = (bf16[512,4096]{1,0:T(8,128)(2,1)S(1)}, bf16[512,4096]{1,0:T(8,128)(2,1)}, u32[]{:S(2)}) copy-start(bf16[512,4096]{1,0:T(8,128)(2,1)} %all-gather.9.cloned.1.call-done) | copy-start | bytes 12582916
  179.5 6.4 %collective-permute-start.3 = (bf16[128,512]{1,0:T(8,128)(2,1)S(1)}, bf16[128,512]{1,0:T(8,128)(2,1)S(1)}, u32[]{:S(2)}, u32[]{:S(2)}) collective-permute-start(bf16[128,512]{1,0:T(8,128)(2,1)S(1)} %shard_map.112), channel_id=1, source_target_pairs={{0,1},{1,0},{2,3},{3,2},{4,5},{5,4},{6,7},{7,6},{8,9},{9,8},{10,11... | collective-permute-start | bytes 393224 | tf_op jit(solution)/shard_map/ppermute | solution.py:265
  181.4 2.2 %copy-start.2 = (bf16[512,4096]{1,0:T(8,128)(2,1)S(1)}, bf16[512,4096]{1,0:T(8,128)(2,1)}, u32[]{:S(2)}) copy-start(bf16[512,4096]{1,0:T(8,128)(2,1)} %all-gather.9.cloned.1.call-done) | copy-start | bytes 12582916
Sparse Core Ops, SparseCore 0:
  11.0 52.3 all-gather.4
Sparse Core Ops, SparseCore 1:
  87.8 28.3 all-gather.6
  118.2 50.7 all-gather.8

commit v3 on v1

--- a/solution.py
+++ b/solution.py
@@ -82,9 +82,14 @@
     forward = (forward_ref[0], forward_ref[1])
     backward = (backward_ref[0], backward_ref[1])
     cosine, sine = twist_ref[0], twist_ref[1]
+    _, chips, chip_rows = source_ref.shape
+    starts = range(0, chip_rows, SIDE)
     for channel in range(source_ref.shape[0]):
         signal = spectrum(
-            source_ref[channel].astype(jnp.float32), columns, forward, cosine, sine
+            jnp.concatenate(
+                [source_ref[channel, :, start : start + SIDE] for start in starts], axis=0
+            ).astype(jnp.float32),
+            columns, forward, cosine, sine,
         )
         sig_real, sig_imag = signal[:, :SIDE], signal[:, SIDE:]
         taps = spec_ref[channel]
@@ -96,7 +101,9 @@
         back = times_table(product, backward)
         real, imag = back[:, :SIDE], back[:, SIDE:]
         turned = jnp.concatenate([real * cosine - imag * sine, imag * cosine + real * sine], axis=0)
-        out_ref[channel] = table_times(rows, turned).astype(out_ref.dtype)
+        result = table_times(rows, turned).astype(out_ref.dtype)
+        for index, start in enumerate(starts):
+            out_ref[channel, :, start : start + SIDE] = result[index * chips : (index + 1) * chips]
 
 
 def filter_spectrum(blocks):
@@ -110,7 +117,13 @@
 
 
 def long_convolution(blocks, spec):
-    columns, rows, forward, backward, twist = (jnp.asarray(table) for table in tables())
+    columns, rows, forward, backward, twist = tables()
+    chips, parts = blocks.shape[1], blocks.shape[2] // SIDE
+    order = (np.arange(chips)[None, :] * parts + np.arange(parts)[:, None]).reshape(-1)
+    columns, rows = columns[:, :, order], rows[:, order, :]
+    columns, rows, forward, backward, twist = (
+        jnp.asarray(table) for table in (columns, rows, forward, backward, twist)
+    )
     return pl.pallas_call(
         conv_kernel,
         out_shape=jax.ShapeDtypeStruct(blocks.shape, BF),
@@ -194,9 +207,9 @@
     sent, spec = lax.optimization_barrier((sent, spec))
     later, _ = lax.optimization_barrier((mine, sent))
     blocks = exchange(sent, "seq", chip_groups)
-    blocks = blocks.transpose(1, 0, 2).reshape(own, SIDE, SIDE)
+    blocks = blocks.transpose(1, 0, 2)
     result = long_convolution(blocks, spec)
-    result = result.reshape(own, chips, chip_rows).transpose(1, 0, 2)
+    result = result.transpose(1, 0, 2)
     long_conv = exchange(result, "seq", chip_groups).reshape(half, chip_rows)
 
     strip = lax.dynamic_slice_in_dim(later, rows + tp_index * piece, piece, 0)

time: 195 us -> 196 us (level)
    unnamed x32 -> x34, local copies, waits for them, and re-layouts: 4.83 us -> 4.97 us
where the time goes in v3:
time: 196 us; the launch traced here: 195 us
  blocking collectives  65.2 us (33%)
  starting transfers between devices  41.3 us (21%)
  waiting for transfers between devices  33.1 us (17%)
  local copies, waits for them, and re-layouts  17.7 us (9%)
  between operations  15.3 us (8%)
  matrix products  15.1 us (8%)
  other arithmetic  4.05 us (2%)
  Pallas kernels  3.16 us (2%)
    all_to_all x2, blocking collectives, exchange(): lax.all_to_all(value, axis, split_axis=0, concat_axis=0, tiled=True, axis...  65.2 us
    all_to_all x4, starting transfers between devices, exchange(): lax.all_to_all(value, axis, split_axis=0, concat_axis=0, tiled=True, axis...  32.2 us
    all_to_all x4, waiting for transfers between devices, exchange(): lax.all_to_all(value, axis, split_axis=0, concat_axis=0, tiled=True, axis...  20.3 us
    all_gather x1, waiting for transfers between devices, body(): lax.all_gather(strip.reshape(piece, tp_count, features), 'seq', axis=0, a...  8.39 us
    ppermute x2, starting transfers between devices, project(): lax.ppermute(lower[rows - rim:], 'seq', [(i, i + 2) for i in range(seq_co...  6.38 us
    dot_general x2, matrix products, project(): first = jnp.dot(mine, table, preferred_element_type=jnp.float32)[:rows]  6.28 us
    dot_general x2, matrix products, project(): second = jnp.dot(theirs, table, preferred_element_type=jnp.float32)[:rows]  5.77 us
    unnamed x34, local copies, waits for them, and re-layouts  4.97 us
  transfers between devices with their start and end apart: 10, of which 6 were waited for; matrix products, arithmetic and copies ran while one was open for 14% of the time, Pallas kernels for 2%

profile of v3, /device:TPU:1, one launch (start us, length us, event | category | flops | bytes accessed | tf_op | source)
XLA Modules:
  0.0 194.8 jit_solution(17331393975189268319)
XLA Ops:
  7.4 1.6 copy-done
  9.1 1.7 pad_maximum_fusion.1
  10.8 0.9 reshape.64
  11.9 0.1 broadcast_in_dim.18
  12.1 34.6 %all_to_all.30 = bf16[16,64,384]{2,1,0:T(8,128)(2,1)S(1)} all-to-all(bf16[16,64,384]{2,1,0:T(8,128)(2,1)S(1)} %bitcast.60), channel_id=1, replica_groups={{0,8,16,24,32,40,48,56,64,72,80,88,96,104,112,120},{128,136,144,152,160..., dimensions={0} | all-to-all | bytes 1572864 | tf_op jit(solution)/shard_map/all_to_all | solution.py:151
  46.7 0.1 broadcast_in_dim.19
  46.8 30.6 %all_to_all.31 = bf16[4,1024,256]{2,1,0:T(8,128)(2,1)} all-to-all(bf16[4,1024,256]{2,1,0:T(8,128)(2,1)S(1)} %broadcast_in_dim.19), channel_id=1, replica_groups={{0,128,256,384},{8,136,264,392},{16,144,272,400},{24,152,280,408},{32,1..., dimensions={0} | all-to-all | bytes 4194304 | tf_op jit(solution)/shard_map/all_to_all | solution.py:151
  77.4 2.6 %collective-permute-start = (bf16[384,4096]{1,0:T(8,128)(2,1)}, bf16[384,4096]{1,0:T(8,128)(2,1)}, u32[]{:S(2)}, u32[]{:S(2)}) collective-permute-start(bf16[384,4096]{1,0:T(8,128)(2,1)} %all-gather.4.cloned.1.call-done), channel_id=1, source_target_pairs={{0,8},{8,0},{16,24},{24,16},{32,40},{40,32},{48,56},{56,48},{64,72... | collective-permute-start | bytes 9437192 | tf_op jit(solution)/shard_map/ppermute | solution.py:156
  80.1 0.1 copy.36
  80.3 0.7 copy.37
  81.0 4.2 %all-to-all-start.2 = ((f32[64,4,256]{2,1,0:T(4,128)}), f32[64,4,256]{2,1,0:T(4,128)S(1)}, u32[]{:S(2)}, u32[]{:S(2)}) async-start(f32[64,4,256]{2,1,0:T(4,128)} %bitcast.13), calls=%async_computation.2 | async-start | bytes 524288 | tf_op jit(solution)/shard_map/all_to_all | solution.py:151
  85.2 0.7 slice.106
  86.0 3.1 %fusion.2 = f32[256,256]{1,0:T(8,128)S(1)} fusion(bf16[4096,256]{1,0:T(8,128)(2,1)} %bitcast.61, bf16[384,4096]{1,0:T(8,128)(2,1)} %all-gather.4.cloned.1.call-done), kind=kOutput, calls=%fused_computation.2 | convolution fusion | flops 536870912 | bytes 4456448 | tf_op jit(solution)/shard_map/dot_general | solution.py:190
  89.2 3.1 %broadcast_select_fusion.1 = (f32[256,256]{1,0:T(8,128)}, f32[256,256]{1,0:T(8,128)S(1)}) fusion(f32[256,256]{1,0:T(8,128)S(1)} %fusion.2, pred[]{:T(512)S(6)} %eq.6, bf16[4096,256]{1,0:T(8,128)(2,1)S(1)} %bitcast.62, bf16[384,4096]{1,0:T(8,128)(2,1)} %collective-permute-done), kind=kOutput, calls=%fused_computation.30 | convolution fusion | flops 537001984 | bytes 4980737 | tf_op jit(solution)/shard_map/dot_general | solution.py:191
  92.3 3.2 %collective-permute-start.1 = (f32[2,256]{1,0:T(2,128)S(1)}, f32[2,256]{1,0:T(2,128)S(1)}, u32[]{:S(2)}, u32[]{:S(2)}) collective-permute-start(f32[2,256]{1,0:T(2,128)S(1)} %slice.101), channel_id=1, source_target_pairs={{0,16},{8,24},{16,32},{24,40},{32,48},{40,56},{48,64},{56,72},{64,... | collective-permute-start | bytes 6152 | tf_op jit(solution)/shard_map/ppermute | solution.py:194
  95.4 0.7 fusion.18
  96.2 0.9 all-to-all-done.2
  97.2 0.7 shard_map.118.spec_ref
  98.0 1.1 pad_maximum_fusion
  99.1 0.1 fusion.9
  99.2 0.8 copy-done.7
  100.0 0.1 copy.35
  100.2 0.7 reshape.68
  100.9 0.9 constant_dynamic-slice_fusion.3
  101.8 0.7 copy.45
  102.5 9.3 %all-to-all-start.3 = ((bf16[32,4,512]{2,1,0:T(4,128)(2,1)}), bf16[32,4,512]{2,1,0:T(4,128)(2,1)S(1)}, u32[]{:S(2)}, u32[]{:S(2)}) async-start(bf16[32,4,512]{2,1,0:T(4,128)(2,1)} %reshape.68), calls=%async_computation.3 | async-start | bytes 262144 | tf_op jit(solution)/shard_map/all_to_all | solution.py:151
  111.8 4.3 %all-gather.6.cloned.1.call-done = bf16[4096,128]{1,0:T(8,128)(2,1)} async-done(((bf16[1024,128]{1,0:T(8,128)(2,1)}), bf16[4096,128]{1,0:T(8,128)(2,1)}) %all-gather.6.cloned.1.call-update) | async-done | bytes 1048592 | tf_op jit(solution)/shard_map/all_gather | solution.py:171
  116.2 3.2 %fusion = f32[256,128]{1,0:T(8,128)} fusion(bf16[4096,128]{1,0:T(8,128)(2,1)} %all-gather.6.cloned.1.call-done, bf16[384,4096]{1,0:T(8,128)(2,1)} %all-gather.4.cloned.1.call-done), kind=kOutput, calls=%fused_computation | convolution fusion | flops 268435456 | bytes 3276800 | tf_op jit(solution)/shard_map/dot_general | solution.py:190
  119.4 1.7 all-to-all-done.3
  121.1 0.9 copy-done.5
  122.0 0.9 copy-done.6
  122.9 2.4 %shard_map.119 = bf16[4,32,512]{2,1,0:T(8,128)(2,1)S(1)} custom-call(bf16[4,32,512]{2,1,0:T(8,128)(2,1)S(1)} %bitcast.56, f32[4,128,256]{2,1,0:T(8,128)S(1)} %shard_map.118.spec_ref, bf16[2,256,128]{2,1,0:T(8,128)(2,1)S(1)} %copy-done.5, bf16[2,128,256]{2,1,0:T(8,128)(2,1)S(1)} %copy-done.6, bf16[2,256,256]{2,1,0:T(8,128)(2,1)S(1)} %copy-done.1, ...), custom_call_target="tpu_custom_call" | custom-call | tf_op jit(solution)/shard_map/pallas_call | solution.py:127
  125.4 0.7 copy.40
  126.1 8.5 %all-to-all-start.4 = ((bf16[32,4,512]{2,1,0:T(4,128)(2,1)}), bf16[32,4,512]{2,1,0:T(4,128)(2,1)S(1)}, u32[]{:S(2)}, u32[]{:S(2)}) async-start(bf16[32,4,512]{2,1,0:T(4,128)(2,1)} %copy.40), calls=%async_computation.4 | async-start | bytes 262144 | tf_op jit(solution)/shard_map/all_to_all | solution.py:151
  134.6 2.7 %broadcast_select_fusion.3 = (f32[256,128]{1,0:T(8,128)S(1)}, f32[256,128]{1,0:T(8,128)S(1)}) fusion(f32[256,128]{1,0:T(8,128)} %fusion, pred[]{:T(512)S(6)} %eq.6, bf16[4096,128]{1,0:T(8,128)(2,1)} %all-gather.6.cloned.1.call-done, bf16[384,4096]{1,0:T(8,128)(2,1)} %collective-permute-done), kind=kOutput, calls=%fused_computation.33 | convolution fusion | flops 268500992 | bytes 3538945 | tf_op jit(solution)/shard_map/dot_general | solution.py:191
  137.3 3.2 %collective-permute-start.2 = (f32[2,128]{1,0:T(2,128)S(1)}, f32[2,128]{1,0:T(2,128)S(1)}, u32[]{:S(2)}, u32[]{:S(2)}) collective-permute-start(f32[2,128]{1,0:T(2,128)S(1)} %slice.107), channel_id=1, source_target_pairs={{0,16},{8,24},{16,32},{24,40},{32,48},{40,56},{48,64},{56,72},{64,... | collective-permute-start | bytes 3080 | tf_op jit(solution)/shard_map/ppermute | solution.py:194
  140.6 0.8 fusion.20
  141.4 0.7 dynamic_slice.14
  142.1 1.8 all-to-all-done.4
  143.9 0.1 copy.41
  144.0 1.0 fusion.14
  145.0 0.1 copy.42
  145.2 1.1 broadcast_in_dim.20
  146.2 10.2 %all-to-all-start.5 = ((bf16[16,128,256]{2,1,0:T(8,128)(2,1)}), bf16[16,128,256]{2,1,0:T(8,128)(2,1)S(1)}, u32[]{:S(2)}, u32[]{:S(2)}) async-start(bf16[16,128,256]{2,1,0:T(8,128)(2,1)} %bitcast.22), calls=%async_computation.5 | async-start | bytes 2097152 | tf_op jit(solution)/shard_map/all_to_all | solution.py:151
  156.5 8.4 %all-gather.8.cloned.1.call-done = bf16[16,16,8,512]{3,2,1,0:T(8,128)(2,1)} async-done(((bf16[1,16,8,512]{3,2,1,0:T(8,128)(2,1)}), bf16[16,16,8,512]{3,2,1,0:T(8,128)(2,1)}) %all-gather.8.cloned.1.call-update) | async-done | bytes 2097168 | tf_op jit(solution)/shard_map/all_gather | solution.py:216
  164.8 3.6 %copy.43 = bf16[16,16,8,512]{3,1,0,2:T(8,128)(2,1)} copy(bf16[16,16,8,512]{3,2,1,0:T(8,128)(2,1)} %all-gather.8.cloned.1.call-done) | data formatting | bytes 4194304 | tf_op jit(solution)/shard_map/all_gather | solution.py:216
  168.5 15.9 %all-to-all-done.5 = bf16[16,128,256]{2,1,0:T(8,128)(2,1)S(1)} async-done(((bf16[16,128,256]{2,1,0:T(8,128)(2,1)}), bf16[16,128,256]{2,1,0:T(8,128)(2,1)S(1)}, u32[]{:S(2)}, u32[]{:S(2)}) %all-to-all-start.5) | async-done | bytes 1048608 | tf_op jit(solution)/shard_map/all_to_all | solution.py:151
  184.4 3.0 %convolution_convert_fusion = bf16[256,512]{1,0:T(8,128)(2,1)} fusion(bf16[2048,256]{1,0:T(8,128)(2,1)S(1)} %bitcast.64, bf16[2048,512]{1,0:T(8,128)(2,1)} %bitcast.63), kind=kOutput, calls=%fused_computation.8 | convolution fusion | flops 537001984 | bytes 3407872 | tf_op jit(solution)/shard_map/dot_general | solution.py:227
  (53 shorter events, 0.8 us)
Async XLA Ops:
  7.4 1.6 copy-start
  7.4 70.1 %all-gather.4.cloned.1.call-start = ((), (), s32[]{:S(2)}) async-start(), calls=%async_computation.6 | async-start | bytes 3538944 | tf_op jit(solution)/shard_map/all_gather | solution.py:162
  46.8 33.3 %copy-start.14 = (f32[256,256]{1,0:T(8,128)S(1)}, f32[256,256]{1,0:T(8,128)}, u32[]{:S(2)}) copy-start(f32[256,256]{1,0:T(8,128)} %param.15) | copy-start | bytes 786436
  77.4 11.7 %collective-permute-start = (bf16[384,4096]{1,0:T(8,128)(2,1)}, bf16[384,4096]{1,0:T(8,128)(2,1)}, u32[]{:S(2)}, u32[]{:S(2)}) collective-permute-start(bf16[384,4096]{1,0:T(8,128)(2,1)} %all-gather.4.cloned.1.call-done), channel_id=1, source_target_pairs={{0,8},{8,0},{16,24},{24,16},{32,40},{40,32},{48,56},{56,48},{64,72... | collective-permute-start | bytes 9437192 | tf_op jit(solution)/shard_map/ppermute | solution.py:156
  81.0 16.1 %all-to-all-start.2 = ((f32[64,4,256]{2,1,0:T(4,128)}), f32[64,4,256]{2,1,0:T(4,128)S(1)}, u32[]{:S(2)}, u32[]{:S(2)}) async-start(f32[64,4,256]{2,1,0:T(4,128)} %bitcast.13), calls=%async_computation.2 | async-start | bytes 524288 | tf_op jit(solution)/shard_map/all_to_all | solution.py:151
  85.2 31.0 %all-gather.6.cloned.1.call-start = ((), (), s32[]{:S(2)}) async-start(), calls=%async_computation.7 | async-start | bytes 1310720 | tf_op jit(solution)/shard_map/all_gather | solution.py:171
  86.0 78.9 %all-gather.8.cloned.1.call-start = ((), (), s32[]{:S(2)}) async-start(), calls=%async_computation.8 | async-start | bytes 2228224 | tf_op jit(solution)/shard_map/all_gather | solution.py:216
  86.0 3.1 %copy-start.9 = (bf16[4,1024,256]{2,1,0:T(8,128)(2,1)S(1)}, bf16[4,1024,256]{2,1,0:T(8,128)(2,1)}, u32[]{:S(2)}) copy-start(bf16[4,1024,256]{2,1,0:T(8,128)(2,1)} %all_to_all.31) | copy-start | bytes 6291460
  89.1 8.0 %copy-start.1 = (bf16[2,256,256]{2,1,0:T(8,128)(2,1)S(1)}, bf16[2,256,256]{2,1,0:T(8,128)(2,1)}, u32[]{:S(2)}) copy-start(bf16[2,256,256]{2,1,0:T(8,128)(2,1)} %constant.53.clone.forward_ref) | copy-start | bytes 786436
  89.1 8.0 %copy-start.2 = (f32[2,128,128]{2,1,0:T(8,128)S(1)}, f32[2,128,128]{2,1,0:T(8,128)}, u32[]{:S(2)}) copy-start(f32[2,128,128]{2,1,0:T(8,128)} %constant.54.clone.twist_ref) | copy-start | bytes 393220
  89.2 8.0 %copy-start.4 = (bf16[2,256,128]{2,1,0:T(8,128)(2,1)S(1)}, bf16[2,256,128]{2,1,0:T(8,128)(2,1)}, u32[]{:S(2)}) copy-start(bf16[2,256,128]{2,1,0:T(8,128)(2,1)} %constant.52.clone.columns_ref) | copy-start | bytes 393220
  92.3 4.9 %copy-start.10 = (f32[256,256]{1,0:T(8,128)}, f32[256,256]{1,0:T(8,128)S(1)}, u32[]{:S(2)}) copy-start(f32[256,256]{1,0:T(8,128)S(1)} %get-tuple-element.16) | copy-start | bytes 786436
  92.3 5.7 %collective-permute-start.1 = (f32[2,256]{1,0:T(2,128)S(1)}, f32[2,256]{1,0:T(2,128)S(1)}, u32[]{:S(2)}, u32[]{:S(2)}) collective-permute-start(f32[2,256]{1,0:T(2,128)S(1)} %slice.101), channel_id=1, source_target_pairs={{0,16},{8,24},{16,32},{24,40},{32,48},{40,56},{48,64},{56,72},{64,... | collective-permute-start | bytes 6152 | tf_op jit(solution)/shard_map/ppermute | solution.py:194
  97.2 1.9 copy-start.11
  97.2 1.9 copy-start.12
  99.2 0.8 copy-start.7
  102.5 18.6 %all-to-all-start.3 = ((bf16[32,4,512]{2,1,0:T(4,128)(2,1)}), bf16[32,4,512]{2,1,0:T(4,128)(2,1)S(1)}, u32[]{:S(2)}, u32[]{:S(2)}) async-start(bf16[32,4,512]{2,1,0:T(4,128)(2,1)} %reshape.68), calls=%async_computation.3 | async-start | bytes 262144 | tf_op jit(solution)/shard_map/all_to_all | solution.py:151
  111.8 9.3 %copy-start.3 = (bf16[2,256,256]{2,1,0:T(8,128)(2,1)S(1)}, bf16[2,256,256]{2,1,0:T(8,128)(2,1)}, u32[]{:S(2)}) copy-start(bf16[2,256,256]{2,1,0:T(8,128)(2,1)} %constant.57.clone.backward_ref) | copy-start | bytes 786436
  121.1 0.9 copy-start.5
  122.0 0.9 copy-start.6
  126.1 17.7 %all-to-all-start.4 = ((bf16[32,4,512]{2,1,0:T(4,128)(2,1)}), bf16[32,4,512]{2,1,0:T(4,128)(2,1)S(1)}, u32[]{:S(2)}, u32[]{:S(2)}) async-start(bf16[32,4,512]{2,1,0:T(4,128)(2,1)} %copy.40), calls=%async_computation.4 | async-start | bytes 262144 | tf_op jit(solution)/shard_map/all_to_all | solution.py:151
  134.6 6.8 %copy-start.15 = (f32[256]{0:T(256)S(1)}, f32[256]{0:T(256)}, u32[]{:S(2)}) copy-start(f32[256]{0:T(256)} %param.16) | copy-start | bytes 3076
  134.6 9.4 %copy-start.8 = (f32[256,512]{0,1:T(8,128)S(1)}, f32[256,512]{0,1:T(8,128)}, u32[]{:S(2)}) copy-start(f32[256,512]{0,1:T(8,128)} %copy-done.7) | copy-start | bytes 1572868
  137.3 6.5 %copy-start.13 = (f32[256,128]{1,0:T(8,128)}, f32[256,128]{1,0:T(8,128)S(1)}, u32[]{:S(2)}) copy-start(f32[256,128]{1,0:T(8,128)S(1)} %get-tuple-element.17) | copy-start | bytes 393220
  137.3 4.7 %collective-permute-start.2 = (f32[2,128]{1,0:T(2,128)S(1)}, f32[2,128]{1,0:T(2,128)S(1)}, u32[]{:S(2)}, u32[]{:S(2)}) collective-permute-start(f32[2,128]{1,0:T(2,128)S(1)} %slice.107), channel_id=1, source_target_pairs={{0,16},{8,24},{16,32},{24,40},{32,48},{40,56},{48,64},{56,72},{64,... | collective-permute-start | bytes 3080 | tf_op jit(solution)/shard_map/ppermute | solution.py:194
  146.2 38.2 %all-to-all-start.5 = ((bf16[16,128,256]{2,1,0:T(8,128)(2,1)}), bf16[16,128,256]{2,1,0:T(8,128)(2,1)S(1)}, u32[]{:S(2)}, u32[]{:S(2)}) async-start(bf16[16,128,256]{2,1,0:T(8,128)(2,1)} %bitcast.22), calls=%async_computation.5 | async-start | bytes 2097152 | tf_op jit(solution)/shard_map/all_to_all | solution.py:151
Sparse Core Ops, SparseCore 0:
  11.0 52.3 all-gather.3
Sparse Core Ops, SparseCore 1:
  87.7 28.4 all-gather.5
  118.2 46.6 all-gather.7
